TPU v7x, 256 devices: a whole 4x4x8 slice. The times are simulated.
256 devices in a mesh: aux: 32 (over y, x, core), occ: 8 (over z).
Axes of the slice: x: 4, y: 4, z: 8, core: 2. Of those that a mesh axis runs over, the one named last changes fastest.
Arguments:
- integrals: bfloat16 [256, 8, 48, 4096], P(('aux', 'occ')), may hold values from -1 to 1
- mu_shells: int32 [256, 8], P(('aux', 'occ')), may hold values from 0 to 63
- nu_shells: int32 [256, 8], P(('aux', 'occ')), may hold values from 0 to 21
- block_count: int32 [256], P(('aux', 'occ')), may hold values from 1 to 8, as said below
- occ_coeffs: bfloat16 [4096, 32], replicated
- vir_coeffs: bfloat16 [1408, 1600], replicated, may hold values from -0.15625 to 0.15625
- occ_order: int32 [32], replicated, may hold values from 0 to 31, each once
- occ_energies: float32 [32], replicated, may hold values from -2 to -0.5
- vir_energies: float32 [1600], replicated, may hold values from 0.015 to 25
Outputs:
- amplitudes: bfloat16 [32, 1600, 1600], P('aux', 'occ')
- pair_energy: float32 [32], P('aux')
Inputs may be any that keep to these rules, and one draw needn't show every extreme that they name: Only the first block_count[s] entries of slab s's block lists and integrals are screened in; some slab has all 8 slots in use.
All inputs are finite; a program needn't handle non-finite values.
Results may differ from a plain program's by a relative error of at most 0.017.
Values may be sent and summed in bfloat16 or wider, within the bound.
A program may use at most 128 MiB of HBM per device.

v0:
```python
import jax
import jax.numpy as jnp
from jax import lax
from jax.sharding import PartitionSpec as P

NAO = 4096
SHELL = 64
NU_W = 1408
NVIR = 1600


def shifted(value, axis, steps):
    count = lax.axis_size(axis)
    pairs = [(source, (source + steps) % count) for source in range(count)]
    return lax.ppermute(value, axis, pairs)


def half_block(integrals, mu_shells, nu_shells, block_count, occ_coeffs, occ_order):
    occ_count = occ_order.shape[0]
    slots = integrals.shape[1]
    slab = integrals.shape[2]
    picker = (jnp.arange(occ_count)[:, None] == occ_order[None, :]).astype(jnp.bfloat16)
    chosen = jnp.dot(occ_coeffs, picker, preferred_element_type=jnp.float32).astype(jnp.bfloat16)
    shell_rows = chosen.reshape(NAO // SHELL, SHELL, occ_count)
    rows = jnp.take(shell_rows, mu_shells[0], axis=0)
    blocks = integrals[0].reshape(slots, slab, SHELL, SHELL)
    parts = jnp.einsum("kpmn,kmi->kpin", blocks, rows, preferred_element_type=jnp.float32)
    live = (jnp.arange(slots) < block_count[0]).astype(jnp.float32)
    place = (nu_shells[0][:, None] == jnp.arange(NU_W // SHELL)[None, :]).astype(
        jnp.float32
    ) * live[:, None]
    half = jnp.einsum("kpin,ks->pisn", parts, place, precision=lax.Precision.HIGHEST)
    return half.reshape(slab, occ_count, NU_W).astype(jnp.bfloat16)


def widen(half, vir_coeffs):
    leading = half.shape[:-1]
    result = jnp.dot(half.reshape(-1, NU_W), vir_coeffs, preferred_element_type=jnp.float32).astype(
        jnp.bfloat16
    )
    return result.reshape(leading + (NVIR,))


def local(
    integrals,
    mu_shells,
    nu_shells,
    block_count,
    occ_coeffs,
    vir_coeffs,
    occ_order,
    occ_energies,
    vir_energies,
):
    occ_count = occ_order.shape[0]
    half = half_block(integrals, mu_shells, nu_shells, block_count, occ_coeffs, occ_order)
    ri_rows = widen(half, vir_coeffs)
    mine = lax.all_to_all(ri_rows, "aux", split_axis=1, concat_axis=0, tiled=True)
    other = shifted(mine, "aux", 1)
    own_rows = mine.reshape(-1, NVIR)
    partner = other.reshape(-1, NVIR)
    width = NVIR // lax.axis_size("occ")
    contract = (((0,), (0,)), ((), ()))
    summed = lax.psum_scatter(
        lax.dot_general(partner, own_rows, contract, preferred_element_type=jnp.float32).astype(
            jnp.bfloat16
        ),
        "occ",
        scatter_dimension=0,
        tiled=True,
    ).astype(jnp.float32)
    swapped = lax.all_to_all(
        summed.astype(jnp.bfloat16), "occ", split_axis=1, concat_axis=0, tiled=True
    ).astype(summed.dtype)
    mirror = jnp.transpose(swapped)
    batch = lax.axis_index("aux")
    chosen_energy = jnp.take(occ_energies, occ_order)
    e_pair = jnp.take(chosen_energy, batch) + jnp.take(chosen_energy, (batch - 1) % occ_count)
    block_energy = lax.dynamic_slice_in_dim(vir_energies, lax.axis_index("occ") * width, width)
    denominator = e_pair - block_energy[:, None] - vir_energies[None, :]
    ratio = summed / denominator
    partial_energy = jnp.sum(ratio * (2.0 * summed - mirror))
    total = lax.psum(partial_energy, "occ")
    energy = (total / (NVIR * NVIR)).reshape(1)
    return (ratio.astype(jnp.bfloat16)[None], energy)


def solution(mesh):
    placed = (
        P(("aux", "occ"), None, None, None),
        P(("aux", "occ"), None),
        P(("aux", "occ"), None),
        P(("aux", "occ")),
        P(),
        P(),
        P(),
        P(),
        P(),
    )
    return jax.shard_map(
        local,
        mesh=mesh,
        in_specs=placed,
        out_specs=(P("aux", "occ", None), P("aux")),
        check_vma=False,
    )
```

profile of v0, /device:TPU:1, one launch (start us, length us, event | category | flops | bytes accessed | tf_op | source)
XLA Modules:
  0.0 348.7 jit_solution(2516786985381490869)
XLA Ops:
  7.2 0.0 copy-start
  7.2 0.0 copy-start.5
  7.2 0.0 reduce-scatter.4.cloned.1.call-start
  7.2 0.7 fusion.18
  7.9 0.7 compare_and_fusion
  8.6 9.6 %reshape_squeeze.3 = bf16[8,48,64,64]{3,2,1,0:T(8,128)(2,1)} reshape(bf16[1,8,48,4096]{3,2,1,0:T(8,128)(2,1)} %param.9) | data formatting | bytes 6291456 | tf_op jit(solution)/shard_map/reshape;squeeze | solution.py:26
  18.2 0.0 copy-done
  18.2 0.0 copy-done.5
  18.2 0.3 fusion.2
  18.5 0.5 reshape.80
  19.1 0.3 copy.18
  20.1 0.6 gather_fusion
  20.6 0.0 copy-start.4
  20.7 3.8 %convolution_bitcast_fusion = f32[8,48,32,64]{3,2,1,0:T(8,128)S(1)} fusion(bf16[8,48,64,64]{3,2,1,0:T(8,128)(2,1)} %reshape_squeeze.3, bf16[8,64,32]{1,2,0:T(8,128)(2,1)S(1)} %gather_fusion, pred[8]{0:T(512)(128)(4,1)S(1)} %compare_and_fusion), kind=kOutput, calls=%fused_computation.9 | convolution fusion | flops 100679680 | bytes 6324232 | tf_op jit(solution)/shard_map/kpmn,kmi->kpin/dot_general | solution.py:27
  24.5 0.0 copy-done.4
  24.5 18.0 %convert_bitcast_fusion = bf16[48,32,22,64]{3,2,1,0:T(8,128)(2,1)} fusion(f32[8,48,32,64]{3,2,1,0:T(8,128)S(1)} %convolution_bitcast_fusion, f32[8]{0:T(128)S(1)} %compare_convert_fusion, s32[8]{0:T(128)S(1)} %bitcast.61), kind=kOutput, calls=%fused_computation.2 | convolution fusion | flops 209781088 | bytes 7471168 | tf_op jit(solution)/shard_map/kpin,ks->pisn/dot_general | solution.py:32
  42.5 12.8 %convert_element_type.50 = bf16[1536,1408]{1,0:T(8,128)(2,1)} reshape(bf16[48,32,22,64]{3,2,1,0:T(8,128)(2,1)} %convert_bitcast_fusion) | data formatting | bytes 8650752 | tf_op jit(solution)/shard_map/convert_element_type | solution.py:33
  55.3 12.6 %convolution_convert_fusion.1 = bf16[1536,1600]{0,1:T(8,128)(2,1)} fusion(bf16[1536,1408]{1,0:T(8,128)(2,1)} %convert_element_type.50, bf16[1408,1600]{0,1:T(8,128)(2,1)} %param.14), kind=kOutput, calls=%fused_computation.4 | convolution fusion | flops 6923059200 | bytes 13746176 | tf_op jit(solution)/shard_map/dot_general | solution.py:38
  67.9 7.6 %copy.20 = bf16[1536,1600]{1,0:T(8,128)(2,1)} copy(bf16[1536,1600]{0,1:T(8,128)(2,1)} %convolution_convert_fusion.1) | data formatting | bytes 9830400 | tf_op jit(solution)/shard_map/convert_element_type | solution.py:38
  75.4 4.1 %copy.21 = bf16[48,32,1600]{2,0,1:T(8,128)(2,1)S(1)} copy(bf16[48,32,1600]{2,1,0:T(8,128)(2,1)} %bitcast.59) | data formatting | bytes 9830400 | tf_op jit(solution)/shard_map/reshape | solution.py:41
  79.5 69.2 %all_to_all.31 = bf16[48,32,1600]{2,0,1:T(8,128)(2,1)} all-to-all(bf16[48,32,1600]{2,0,1:T(8,128)(2,1)S(1)} %copy.21), channel_id=1, replica_groups=mesh['aux'=32,'occ'=8] {'aux'}, dimensions={1} | all-to-all | bytes 9830400 | tf_op jit(solution)/shard_map/all_to_all | solution.py:58
  148.7 7.7 %copy.22 = bf16[1536,1,1600]{0,2,1:T(8,128)(2,1)} copy(bf16[1536,1,1600]{2,0,1:T(8,128)(2,1)} %bitcast.57) | data formatting | bytes 9830400 | tf_op jit(solution)/shard_map/all_to_all | solution.py:58
  156.4 0.6 collective-permute-start
  157.0 53.5 %collective-permute-done = bf16[1536,1,1600]{0,2,1:T(8,128)(2,1)S(1)} collective-permute-done((bf16[1536,1,1600]{0,2,1:T(8,128)(2,1)}, bf16[1536,1,1600]{0,2,1:T(8,128)(2,1)S(1)}, u32[]{:S(2)}, u32[]{:S(2)}) %collective-permute-start) | collective-permute-done | bytes 4915232 | tf_op jit(solution)/shard_map/ppermute | solution.py:15
  210.4 13.1 %convolution_convert_fusion = bf16[1600,1600]{1,0:T(8,128)(2,1)} fusion(bf16[1536,1600]{1,0:T(8,128)(2,1)} %bitcast.58, bf16[1536,1,1600]{0,2,1:T(8,128)(2,1)S(1)} %collective-permute-done), kind=kOutput, calls=%fused_computation.3 | convolution fusion | flops 7866880000 | bytes 14950400 | tf_op jit(solution)/shard_map/dot_general | solution.py:65
  223.6 0.0 copy-start.2
  223.6 0.0 copy-start.3
  223.6 0.0 reduce-scatter.4.cloned.1.call-update
  223.6 69.4 %reduce-scatter.4.cloned.1.call-done = bf16[200,1600]{1,0:T(8,128)(2,1)} async-done(((bf16[1600,1600]{1,0:T(8,128)(2,1)}), bf16[200,1600]{1,0:T(8,128)(2,1)}) %reduce-scatter.4.cloned.1.call-update) | async-done | bytes 640016
  293.0 2.5 all_to_all.27
  295.5 0.0 copy-start.1
  295.5 1.1 copy.23
  296.5 4.0 %all-to-all-start.1 = ((bf16[200,8,200]{2,0,1:T(8,128)(2,1)}), bf16[200,8,200]{2,0,1:T(8,128)(2,1)S(1)}, u32[]{:S(2)}, u32[]{:S(2)}) async-start(bf16[200,8,200]{2,0,1:T(8,128)(2,1)} %copy.23), calls=%async_computation.1 | async-start | bytes 1638400 | tf_op jit(solution)/shard_map/all_to_all | solution.py:72
  300.6 0.0 copy-done.2
  300.6 0.7 gather_fusion.1
  301.3 0.7 fusion.21
  303.3 0.0 copy-done.3
  303.3 0.1 dynamic-slice_subtract_fusion
  303.4 21.5 %all-to-all-done.1 = bf16[200,8,200]{2,0,1:T(8,128)(2,1)S(1)} async-done(((bf16[200,8,200]{2,0,1:T(8,128)(2,1)}), bf16[200,8,200]{2,0,1:T(8,128)(2,1)S(1)}, u32[]{:S(2)}, u32[]{:S(2)}) %all-to-all-start.1) | async-done | bytes 640032 | tf_op jit(solution)/shard_map/all_to_all | solution.py:72
  324.9 0.1 transpose.42
  325.0 0.5 copy.27
  325.5 3.0 fusion.5
  328.5 11.5 %psum.7 = f32[]{:T(128)} all-reduce(f32[]{:T(128)} %get-tuple-element.24), channel_id=1, replica_groups=mesh['aux'=32,'occ'=8] {'occ'}, use_global_device_ids=true, to_apply=%region_2.3 | all-reduce | flops 1 | bytes 8 | tf_op jit(solution)/shard_map/psum | solution.py:83
  340.7 0.0 copy-done.1
  (5 shorter events, 0.0 us)
Async XLA Ops:
  7.2 11.1 %copy-start = (bf16[4096,32]{0,1:T(8,128)(2,1)S(1)}, bf16[4096,32]{0,1:T(8,128)(2,1)}, u32[]{:S(2)}) copy-start(bf16[4096,32]{0,1:T(8,128)(2,1)} %param.13) | copy-start | bytes 786436
  7.2 11.1 %copy-start.5 = (s32[32]{0:T(128)S(1)}, s32[32]{0:T(128)}, u32[]{:S(2)}) copy-start(s32[32]{0:T(128)} %param.15) | copy-start | bytes 388
  7.2 285.8 %reduce-scatter.4.cloned.1.call-start = ((), (), s32[]{:S(2)}) async-start(), calls=%async_computation.3 | async-start | bytes 5990400
  20.6 3.8 %copy-start.4 = (s32[1,8]{1,0:T(1,128)S(1)}, s32[1,8]{1,0:T(1,128)}, u32[]{:S(2)}) copy-start(s32[1,8]{1,0:T(1,128)} %param.11) | copy-start | bytes 100
  156.4 54.1 %collective-permute-start = (bf16[1536,1,1600]{0,2,1:T(8,128)(2,1)}, bf16[1536,1,1600]{0,2,1:T(8,128)(2,1)S(1)}, u32[]{:S(2)}, u32[]{:S(2)}) collective-permute-start(bf16[1536,1,1600]{0,2,1:T(8,128)(2,1)} %copy.22), channel_id=1, source_target_pairs={{0,8},{8,16},{16,24},{24,32},{32,40},{40,48},{48,56},{56,64},{64,7... | collective-permute-start | bytes 14745608 | tf_op jit(solution)/shard_map/ppermute | solution.py:15
  223.6 77.1 %copy-start.2 = (f32[32]{0:T(128)S(1)}, f32[32]{0:T(128)}, u32[]{:S(2)}) copy-start(f32[32]{0:T(128)} %param.16) | copy-start | bytes 388
  223.6 79.8 %copy-start.3 = (f32[1600]{0:T(1024)S(1)}, f32[1600]{0:T(1024)}, u32[]{:S(2)}) copy-start(f32[1600]{0:T(1024)} %param.17) | copy-start | bytes 19204
  295.5 45.2 %copy-start.1 = (bf16[4096,32]{0,1:T(8,128)(2,1)S(1)}, bf16[4096,32]{0,1:T(8,128)(2,1)}, u32[]{:S(2)}) copy-start(bf16[4096,32]{0,1:T(8,128)(2,1)} %param.13) | copy-start | bytes 786436
  296.5 28.3 %all-to-all-start.1 = ((bf16[200,8,200]{2,0,1:T(8,128)(2,1)}), bf16[200,8,200]{2,0,1:T(8,128)(2,1)S(1)}, u32[]{:S(2)}, u32[]{:S(2)}) async-start(bf16[200,8,200]{2,0,1:T(8,128)(2,1)} %copy.23), calls=%async_computation.1 | async-start | bytes 1638400 | tf_op jit(solution)/shard_map/all_to_all | solution.py:72
Sparse Core Ops, SparseCore 0:
  223.7 69.2 reduce-scatter.3
where the time goes:
time: 353 us; the launch traced here: 349 us
  waiting for transfers between devices  144 us (41%)
  blocking collectives  80.7 us (23%)
  local copies, waits for them, and re-layouts  48.6 us (14%)
  matrix products  47.8 us (14%)
  between operations  17.9 us (5%)
  starting transfers between devices  4.65 us (1%)
  other arithmetic  4.6 us (1%)
    unnamed x2, waiting for transfers between devices  69.4 us
    all_to_all x1, blocking collectives, local(): lax.all_to_all(ri_rows, 'aux', split_axis=1, concat_axis=0, tiled=True)  69.2 us
    ppermute x1, waiting for transfers between devices, shifted(): return lax.ppermute(value, axis, pairs)  53.5 us
    all_to_all x1, waiting for transfers between devices, local(): lax.all_to_all(summed.astype(jnp.bfloat16), 'occ', split_axis=1, concat_a...  21.5 us
    dot_general x1, matrix products, half_block(): jnp.einsum('kpin,ks->pisn', parts, place, precision=lax.Precision.HIGHEST)  18 us
    dot_general x1, matrix products, local(): lax.dot_general(partner, own_rows, contract, preferred_element_type=jnp.f...  13.1 us
    convert_element_type x1, local copies, waits for them, and re-layouts, half_block(): return half.reshape(slab, occ_count, NU_W).astype(jnp.bfloat16)  12.8 us
    dot_general x1, matrix products, widen(): jnp.dot(half.reshape(-1, NU_W), vir_coeffs, preferred_element_type=jnp.fl...  12.6 us
  transfers between devices with their start and end apart: 3, of which 3 were waited for; matrix products, arithmetic and copies ran while one was open for 0% of the time, Pallas kernels for 0%

commit v1 on v0

v1 whole, which is shorter than its diff:
```python
import functools

import jax
import jax.numpy as jnp
from jax import lax
from jax.experimental import pallas as pl
from jax.experimental.pallas import tpu as pltpu
from jax.sharding import PartitionSpec as P

SHELL = 64
LANE = 128
ROWS = 16
MESH = pl.DeviceIdType.MESH
F32 = jnp.float32
BF16 = jnp.bfloat16
NT = (((1,), (1,)), ((), ()))


def left_half(shape):
    return lax.broadcasted_iota(jnp.int32, shape, len(shape) - 1) < SHELL


def half_kernel(slots, occ_count, mu_ref, x_ref, occ_ref, order_ref, merge_ref, out_ref, tall, lhs, spread, prods):
    lane_tiles = SHELL * SHELL // LANE
    depth = slots * lane_tiles
    wide = slots * occ_count

    @pl.when(pl.program_id(0) == 0)
    def _():
        row = lax.broadcasted_iota(jnp.int32, (SHELL, SHELL), 0)
        col = lax.broadcasted_iota(jnp.int32, (SHELL, SHELL), 1)
        split = (col == 2 * (row % lane_tiles) + row // lane_tiles).astype(F32).astype(BF16)
        picked = lax.broadcasted_iota(jnp.int32, (occ_count, wide), 0) == order_ref[...]
        for k in range(slots):
            start = pl.multiple_of(mu_ref[k] * SHELL, SHELL)
            rows = occ_ref[pl.ds(start, SHELL), :]
            parted = jnp.dot(split, rows, preferred_element_type=F32).astype(BF16)
            picker = jnp.where(picked, merge_ref[k : k + 1, :], 0.0).astype(BF16)
            both = jnp.dot(parted, picker, preferred_element_type=F32)
            tall[k * lane_tiles : (k + 1) * lane_tiles, :] = both[:lane_tiles]
            tall[depth + k * lane_tiles : depth + (k + 1) * lane_tiles, :] = both[lane_tiles:]
        lhs[...] = tall[...].T.astype(BF16)

    @pl.loop(0, slots)
    def _(k):
        for t in range(lane_tiles):
            at = pl.multiple_of((k * lane_tiles + t) * ROWS, ROWS)
            spread[pl.ds(at, ROWS), :] = x_ref[k, :, t * LANE : (t + 1) * LANE].astype(F32)

    half_rows = ROWS // 2
    left = left_half((depth, LANE))
    for r in range(0, half_rows, 2):
        columns = []
        for e in range(2):
            one = spread[pl.ds(r + e, depth, stride=ROWS), :]
            two = spread[pl.ds(r + e + half_rows, depth, stride=ROWS), :]
            low = jnp.where(left, one, pltpu.roll(two, SHELL, 1))
            high = jnp.where(left, pltpu.roll(one, SHELL, 1), two)
            columns.append(jnp.concatenate([low, high], axis=0).astype(BF16))
        both = jnp.dot(lhs[...], jnp.concatenate(columns, axis=1), preferred_element_type=F32)
        for e in range(2):
            prods[(r + e) * wide : (r + e + 1) * wide, :] = both[:, e * LANE : (e + 1) * LANE]

    left = left_half((half_rows, LANE))
    for i in range(occ_count + 1):
        batch = (i - 1) % occ_count
        for q in range(slots // 2):
            one = prods[pl.ds(2 * q * occ_count + batch, half_rows, stride=wide), :]
            two = prods[pl.ds((2 * q + 1) * occ_count + batch, half_rows, stride=wide), :]
            top = jnp.where(left, one, pltpu.roll(two, SHELL, 1))
            low = jnp.where(left, pltpu.roll(one, SHELL, 1), two)
            out_ref[i, :, q * LANE : (q + 1) * LANE] = jnp.concatenate([top, low], axis=0).astype(BF16)


def half_rows_of(integrals, mu, merge, order, occ_coeffs):
    slots, slab, _ = integrals.shape
    nao, occ_count = occ_coeffs.shape
    wide = slots * occ_count
    depth = slots * SHELL * SHELL // LANE
    return pl.pallas_call(
        functools.partial(half_kernel, slots, occ_count),
        grid_spec=pltpu.PrefetchScalarGridSpec(
            num_scalar_prefetch=1,
            grid=(slab // ROWS,),
            in_specs=[
                pl.BlockSpec((slots, ROWS, SHELL * SHELL), lambda p, mu: (0, p, 0)),
                pl.BlockSpec((nao, occ_count), lambda p, mu: (0, 0)),
                pl.BlockSpec((1, wide), lambda p, mu: (0, 0)),
                pl.BlockSpec((slots, wide), lambda p, mu: (0, 0)),
            ],
            out_specs=pl.BlockSpec((occ_count + 1, ROWS, slots * SHELL), lambda p, mu: (0, p, 0)),
            scratch_shapes=[
                pltpu.VMEM((2 * depth, wide), F32),
                pltpu.VMEM((wide, 2 * depth), BF16),
                pltpu.VMEM((depth * ROWS, LANE), F32),
                pltpu.VMEM((ROWS // 2 * wide, LANE), F32),
            ],
        ),
        out_shape=jax.ShapeDtypeStruct((occ_count + 1, slab, slots * SHELL), BF16),
        compiler_params=pltpu.CompilerParams(vmem_limit_bytes=40 * 2**20),
    )(mu, integrals, occ_coeffs, order, merge)


def pair_kernel(
    n_aux,
    n_occ,
    ext_ref,
    meta_ref,
    vir_ref,
    erow_ref,
    eblock_ref,
    eocc_ref,
    order_ref,
    amp_ref,
    energy_ref,
    got,
    metas,
    places,
    tiles,
    half_y,
    half_x,
    vir,
    tall,
    vir_t,
    lhs,
    wide,
    own,
    out_ring,
    in_ring,
    out_tile,
    in_tile,
    ratios,
    part,
    parts,
    local_sem,
    pair_send,
    pair_recv,
    lone_send,
    lone_recv,
    meta_send,
    meta_recv,
    pass_send,
    pass_recv,
    ring_send,
    ring_recv,
    tile_send,
    tile_recv,
    part_send,
    part_recv,
):
    a = lax.axis_index("aux")
    g = lax.axis_index("occ")
    odd = lax.rem(a, 2)
    mate = a + 1 - 2 * odd
    steps = n_aux // 2
    nu_w, nvir = vir.shape
    width = nvir // n_occ
    padded = vir_t.shape[1]
    slab = got.shape[2]
    packs = got.shape[3] // LANE
    nu_tiles = nu_w // LANE

    def aux(step):
        return lax.rem(a + step + 2 * n_aux, n_aux)

    def occ(step):
        return lax.rem(g + step + 2 * n_occ, n_occ)

    barrier = pltpu.get_barrier_semaphore()

    @pl.loop(1, n_aux)
    def _(d):
        pl.semaphore_signal(barrier, inc=1, device_id={"aux": aux(d)}, device_id_type=MESH)

    @pl.loop(1, n_occ)
    def _(d):
        pl.semaphore_signal(barrier, inc=1, device_id={"occ": occ(d)}, device_id_type=MESH)

    load_vir = pltpu.make_async_copy(vir_ref, vir, local_sem.at[0])
    load_vir.start()
    keep = pltpu.make_async_copy(ext_ref.at[pl.ds(a, 2)], got.at[a], local_sem.at[1])
    keep.start()
    pl.semaphore_wait(barrier, n_aux + n_occ - 2)

    def meta_copy(d):
        return pltpu.make_async_remote_copy(
            meta_ref, metas.at[a], meta_send.at[d], meta_recv.at[d], device_id={"aux": aux(d)}, device_id_type=MESH
        )

    def pair_copy(d):
        to = aux(2 * d)
        return pltpu.make_async_remote_copy(
            ext_ref.at[pl.ds(to, 2)], got.at[a], pair_send.at[d], pair_recv.at[d], device_id={"aux": to}, device_id_type=MESH
        )

    def lone_copy(d):
        to = aux(2 * d + 1)
        side = 1 - odd
        return pltpu.make_async_remote_copy(
            ext_ref.at[to + side],
            got.at[a, side],
            lone_send.at[d],
            lone_recv.at[d],
            device_id={"aux": to},
            device_id_type=MESH,
        )

    def pass_copy(d):
        source = aux(-2 * d)
        return pltpu.make_async_remote_copy(
            got.at[source, 1 - odd],
            got.at[source, odd],
            pass_send.at[d],
            pass_recv.at[d],
            device_id={"aux": mate},
            device_id_type=MESH,
        )

    @pl.loop(1, n_aux)
    def _(d):
        meta_copy(d).start()

    lone_copy(0).start()

    @pl.loop(1, steps)
    def _(d):
        pair_copy(d).start()
        lone_copy(d).start()

    metas[a] = meta_ref[...]
    tiles[:, 2 * packs] = jnp.zeros((2, slab, LANE), BF16)

    load_vir.wait()
    for w in range(0, nvir, LANE):
        end = min(w + LANE, nvir)
        tall[w:end, :] = vir[:, w:end].astype(F32).T

    @pl.loop(0, n_occ)
    def _(c):
        rows = tall[pl.ds(pl.multiple_of(c * width, 8), width), :]
        if padded > width:
            rows = jnp.concatenate([rows, jnp.zeros((padded - width, nu_w), F32)], axis=0)
        vir_t[c] = rows.astype(BF16)

    @pl.loop(1, n_aux)
    def _(d):
        meta_copy(d).wait_recv()

    placing = pltpu.make_async_copy(metas, places, local_sem.at[2])
    placing.start()
    placing.wait()

    left = left_half((slab, LANE))

    def spread(source):
        for side in range(2):
            for q in range(packs):
                tile = got[source, side, :, q * LANE : (q + 1) * LANE]
                tiles[side, q] = tile
                tiles[side, packs + q] = pltpu.roll(tile.astype(F32), SHELL, 1).astype(BF16)
        rows = pl.ds(pl.multiple_of(source * slab, ROWS), slab)
        for c in range(nu_tiles):
            first = places[source, 0, 2 * c]
            second = places[source, 0, 2 * c + 1]
            columns = slice(c * LANE, (c + 1) * LANE)
            half_y[rows, columns] = jnp.where(left, tiles[0, first], tiles[0, second])
            half_x[rows, columns] = jnp.where(left, tiles[1, first], tiles[1, second])

    keep.wait()
    pass_copy(0).start()
    spread(a)

    @pl.loop(1, steps)
    def _(d):
        pair_copy(d).wait_recv()
        pass_copy(d).start()
        spread(aux(-2 * d))

    @pl.loop(0, steps)
    def _(d):
        lone_copy(d).wait_recv()
        pass_copy(lax.rem(d + 1 - odd, steps)).wait_recv()
        spread(aux(-2 * d - 1))

    cut = (padded // ROWS + 1) // 2 * ROWS
    spans = (slice(0, cut), slice(cut, padded))
    way = 1 - 2 * odd

    def ring_copy(t, side):
        return pltpu.make_async_remote_copy(
            out_ring.at[t, pl.ds(spans[side].start, spans[side].stop - spans[side].start)],
            in_ring.at[t, pl.ds(spans[side].start, spans[side].stop - spans[side].start)],
            ring_send.at[side, t],
            ring_recv.at[side, t],
            device_id={"occ": occ(way if side == 0 else -way)},
            device_id_type=MESH,
        )

    @pl.loop(0, n_occ)
    def _(t):
        lhs[spans[0], :] = vir_t[occ(-way * (t + 1)), spans[0], :]
        lhs[spans[1], :] = vir_t[occ(way * (t + 1)), spans[1], :]
        for p in range(0, n_aux * slab, 256):
            end = min(p + 256, n_aux * slab)
            wide[:, p:end] = lax.dot_general(lhs[...], half_y[p:end, :], NT, preferred_element_type=F32).astype(BF16)
        for c in range(0, nu_w, 256):
            end = min(c + 256, nu_w)
            own[:, c:end] = jnp.dot(wide[...], half_x[:, c:end], preferred_element_type=F32)
        for side in range(2):
            span = spans[side]

            @pl.when(t == 0)
            def _():
                out_ring[t, span, :] = own[span, :].astype(BF16)

            @pl.when(t > 0)
            def _():
                ring_copy(t - 1, side).wait_recv()
                out_ring[t, span, :] = (own[span, :] + in_ring[t - 1, span, :].astype(F32)).astype(BF16)

            @pl.when(t < n_occ - 1)
            def _():
                ring_copy(t, side).start()

    last = n_occ - 1
    farthest = n_occ // 2

    def tile_step(d):
        return way * (d if d % 2 == 1 else -d)

    def tile_copy(d):
        return pltpu.make_async_remote_copy(
            out_tile.at[d - 1],
            in_tile.at[d - 1],
            tile_send.at[d - 1],
            tile_recv.at[d - 1],
            device_id={"occ": occ(tile_step(d))},
            device_id_type=MESH,
        )

    for d in range(1, farthest + 1):
        out_tile[d - 1] = lax.dot_general(
            vir_t[occ(tile_step(d))], out_ring[last], NT, preferred_element_type=F32
        ).astype(BF16)
        tile_copy(d).start()

    e_pair = eocc_ref[order_ref[a]] + eocc_ref[order_ref[aux(-1)]]
    block_row = jnp.broadcast_to(eblock_ref[g], (8, eblock_ref.shape[2]))
    e_rows = e_pair - block_row.T[:padded, 0:1]

    total = jnp.zeros((8, LANE), F32)

    def folded(values):
        rows, cols = values.shape
        if cols % LANE:
            values = jnp.concatenate([values, jnp.zeros((rows, LANE - cols % LANE), F32)], axis=1)
        result = values[:, :LANE]
        for c in range(LANE, values.shape[1], LANE):
            result = result + values[:, c : c + LANE]
        return jnp.sum(result.reshape(rows // 8, 8, LANE), axis=0)

    for c in range(0, nvir, 256):
        end = min(c + 256, nvir)
        pair = jnp.dot(out_ring[last], vir[:, c:end], preferred_element_type=F32)
        ratio = pair / (e_rows - erow_ref[:, c:end])
        amp_ref[0, :, c:end] = ratio[:width].astype(BF16)
        total = total + folded(ratio * (2.0 * pair))

    def block_ratio(h):
        block = lax.dot_general(out_ring[last], vir_t[h], NT, preferred_element_type=F32)
        return block / (e_rows - eblock_ref[h][:, :padded])

    same = lax.dot_general(vir_t[g], out_ring[last], NT, preferred_element_type=F32)
    total = total - folded(block_ratio(g) * same)
    for d in range(1, farthest + 1):
        ratios[d - 1] = block_ratio(occ(-tile_step(d)))
    for d in range(1, farthest + 1):
        weight = 1.0 if 2 * d == n_occ else 2.0
        tile_copy(d).wait_recv()
        total = total - weight * folded(ratios[d - 1] * in_tile[d - 1].astype(F32))

    part[...] = total

    def part_copy(d):
        return pltpu.make_async_remote_copy(
            part, parts.at[d], part_send.at[d], part_recv.at[d], device_id={"occ": occ(d)}, device_id_type=MESH
        )

    for d in range(1, n_occ):
        part_copy(d).start()
    for d in range(1, n_occ):
        part_copy(d).wait_recv()
        total = total + parts[d]
    energy_ref[0] = jnp.sum(total) / (nvir * nvir)

    for d in range(1, n_occ):
        part_copy(d).wait_send()
    for d in range(1, farthest + 1):
        tile_copy(d).wait_send()

    @pl.loop(0, n_occ - 1)
    def _(t):
        ring_copy(t, 0).wait_send()
        ring_copy(t, 1).wait_send()

    @pl.loop(1, n_aux)
    def _(d):
        meta_copy(d).wait_send()

    lone_copy(0).wait_send()
    pass_copy(0).wait_send()

    @pl.loop(1, steps)
    def _(d):
        pair_copy(d).wait_send()
        lone_copy(d).wait_send()
        pass_copy(d).wait_send()


def pair_results(n_aux, n_occ, ext, meta, vir_coeffs, erow, eblock, occ_energies, occ_order):
    _, slab, packed = ext.shape
    nu_w, nvir = vir_coeffs.shape
    width = nvir // n_occ
    padded = -(-width // ROWS) * ROWS
    aux_rows = n_aux * slab
    farthest = n_occ // 2
    steps = n_aux // 2
    vmem = pl.BlockSpec(memory_space=pltpu.VMEM)
    smem = pl.BlockSpec(memory_space=pltpu.SMEM)
    anywhere = pl.BlockSpec(memory_space=pl.ANY)
    dma = pltpu.SemaphoreType.DMA
    macs = 2 * n_occ * padded * aux_rows * nu_w
    return pl.pallas_call(
        functools.partial(pair_kernel, n_aux, n_occ),
        in_specs=[anywhere, vmem, anywhere, vmem, vmem, smem, smem],
        out_specs=(vmem, smem),
        out_shape=(jax.ShapeDtypeStruct((1, width, nvir), BF16), jax.ShapeDtypeStruct((1,), F32)),
        scratch_shapes=[
            pltpu.VMEM((n_aux, 2, slab, packed), BF16),
            pltpu.VMEM((n_aux, 8, LANE), jnp.int32),
            pltpu.SMEM((n_aux, 8, LANE), jnp.int32),
            pltpu.VMEM((2, 2 * packed // LANE + 1, slab, LANE), BF16),
            pltpu.VMEM((aux_rows, nu_w), BF16),
            pltpu.VMEM((aux_rows, nu_w), BF16),
            pltpu.VMEM((nu_w, nvir), BF16),
            pltpu.VMEM((nvir, nu_w), F32),
            pltpu.VMEM((n_occ, padded, nu_w), BF16),
            pltpu.VMEM((padded, nu_w), BF16),
            pltpu.VMEM((padded, aux_rows), BF16),
            pltpu.VMEM((padded, nu_w), F32),
            pltpu.VMEM((n_occ, padded, nu_w), BF16),
            pltpu.VMEM((n_occ - 1, padded, nu_w), BF16),
            pltpu.VMEM((farthest, padded, padded), BF16),
            pltpu.VMEM((farthest, padded, padded), BF16),
            pltpu.VMEM((farthest, padded, padded), F32),
            pltpu.VMEM((8, LANE), F32),
            pltpu.VMEM((n_occ, 8, LANE), F32),
            dma((3,)),
            dma((steps,)),
            dma((steps,)),
            dma((steps,)),
            dma((steps,)),
            dma((n_aux,)),
            dma((n_aux,)),
            dma((steps,)),
            dma((steps,)),
            dma((2, n_occ - 1)),
            dma((2, n_occ - 1)),
            dma((farthest,)),
            dma((farthest,)),
            dma((n_occ,)),
            dma((n_occ,)),
        ],
        compiler_params=pltpu.CompilerParams(
            collective_id=0, has_side_effects=True, vmem_limit_bytes=60 * 2**20
        ),
        cost_estimate=pl.CostEstimate(flops=2 * macs, bytes_accessed=2 * nu_w * nvir, transcendentals=0),
    )(ext, meta, vir_coeffs, erow, eblock, occ_energies, occ_order)


def local(
    n_aux,
    n_occ,
    integrals,
    mu_shells,
    nu_shells,
    block_count,
    occ_coeffs,
    vir_coeffs,
    occ_order,
    occ_energies,
    vir_energies,
):
    nu_w, nvir = vir_coeffs.shape
    occ_count = occ_order.shape[0]
    slots = integrals.shape[1]
    width = nvir // n_occ
    padded = -(-width // LANE) * LANE
    nu = nu_shells[0]
    slot = jnp.arange(slots, dtype=jnp.int32)
    live = slot < block_count[0]
    alike = (nu[:, None] == nu[None, :]) & live[:, None] & live[None, :]
    first = live & ~jnp.any(alike & (slot[None, :] < slot[:, None]), axis=1)
    merge = jnp.repeat((alike & first[None, :]).astype(F32), occ_count, axis=1)
    order = jnp.tile(occ_order, slots)[None, :]
    shells = jnp.arange(LANE, dtype=jnp.int32)
    found = first[None, :] & (nu[None, :] == shells[:, None])
    place = jnp.where(slot[None, :] % 2 == shells[:, None] % 2, slot[None, :] // 2, slots // 2 + slot[None, :] // 2)
    place = jnp.min(jnp.where(found, place, slots), axis=1)
    meta = jnp.broadcast_to(place[None, :], (8, LANE))
    ext = half_rows_of(integrals[0], mu_shells[0], merge, order, occ_coeffs)
    eblock = jnp.pad(vir_energies.reshape(n_occ, 1, width), ((0, 0), (0, 0), (0, padded - width)), constant_values=1.0)
    return pair_results(n_aux, n_occ, ext, meta, vir_coeffs, vir_energies[None, :], eblock, occ_energies, occ_order)


def solution(mesh):
    placed = (
        P(("aux", "occ"), None, None, None),
        P(("aux", "occ"), None),
        P(("aux", "occ"), None),
        P(("aux", "occ")),
        P(),
        P(),
        P(),
        P(),
        P(),
    )
    return jax.shard_map(
        functools.partial(local, mesh.shape["aux"], mesh.shape["occ"]),
        mesh=mesh,
        in_specs=placed,
        out_specs=(P("aux", "occ", None), P("aux")),
        check_vma=False,
    )
```

time: 353 us -> 167 us (0.47); the launches traced: 349 us -> 167 us
  waiting for transfers between devices: 144 us -> 0 us
  Pallas kernels: 0 us -> 143 us
  blocking collectives: 80.7 us -> 0 us
  matrix products: 47.8 us -> 0 us
  local copies, waits for them, and re-layouts: 48.6 us -> 18.4 us
  between operations: 17.9 us -> 3.02 us
  starting transfers between devices: 4.65 us -> 0 us
    pallas_call x0 -> x2, Pallas kernels: none -> 143 us  [the longest x1 135 us: pair_results(): pl.pallas_call(functools.partial(pair_kernel, n_aux, n_occ), in_specs=[an...]
    unnamed x2 -> x0, waiting for transfers between devices: 69.4 us -> none
    all_to_all x1 -> x0, blocking collectives: 69.2 us -> none  [local(): lax.all_to_all(ri_rows, 'aux', split_axis=1, concat_axis=0, tiled=True)]
    ppermute x1 -> x0, waiting for transfers between devices: 53.5 us -> none  [shifted(): return lax.ppermute(value, axis, pairs)]
    dot_general x5 -> x0, matrix products: 47.8 us -> none  [the longest x1 18 us: half_block(): jnp.einsum('kpin,ks->pisn', parts, place, precision=lax.Precision.HIGHEST)]
    all_to_all x1 -> x0, waiting for transfers between devices: 21.5 us -> none  [local(): lax.all_to_all(summed.astype(jnp.bfloat16), 'occ', split_axis=1, concat_a...]
    convert_element_type x2 -> x0, local copies, waits for them, and re-layouts: 20.3 us -> none  [the longest x1 12.8 us: half_block(): return half.reshape(slab, occ_count, NU_W).astype(jnp.bfloat16)]
    unnamed x12 -> x9, local copies, waits for them, and re-layouts: 0.04 us -> 14.3 us
  transfers between devices with their start and end apart: 3 -> 0, of which waited for: 3 -> 0; matrix products, arithmetic and copies ran while one was open for 0% -> 0% of each run, Pallas kernels for 0% -> 0%
where the time goes in v1:
time: 167 us
  Pallas kernels  143 us (86%)
  local copies, waits for them, and re-layouts  18.4 us (11%)
  between operations  3.02 us (2%)
  other arithmetic  2.5 us (1%)
    pallas_call x1, Pallas kernels, pair_results(): pl.pallas_call(functools.partial(pair_kernel, n_aux, n_occ), in_specs=[an...  135 us
    unnamed x9, local copies, waits for them, and re-layouts  14.3 us
    pallas_call x1, Pallas kernels, half_rows_of(): pl.pallas_call(functools.partial(half_kernel, slots, occ_count), grid_spe...  8.18 us

profile of v1, /device:TPU:1, one launch (start us, length us, event | category | flops | bytes accessed | tf_op | source)
XLA Modules:
  0.0 166.8 jit_solution(9223147521110376654)
XLA Ops:
  1.3 0.9 fusion.1
  2.2 0.7 select_reduce_fusion
  3.0 0.8 and_convert_fusion
  3.8 0.6 broadcast_in_dim.30.meta_ref
  4.4 0.7 tile.2
  5.0 0.1 broadcast_in_dim_tile.3.order_ref
  5.1 1.3 broadcast_in_dim.48.erow_ref
  6.4 0.8 reshape.98
  7.2 0.6 pad.4.eblock_ref
  7.8 0.1 broadcast_in_dim.26
  7.9 0.1 reshape.97.merge_ref
  8.0 1.4 copy.13.occ_ref
  9.4 0.0 copy-start
  9.4 1.9 %copy-done = bf16[1,8,48,4096]{3,2,1,0:T(8,128)(2,1)S(1)} copy-done((bf16[1,8,48,4096]{3,2,1,0:T(8,128)(2,1)S(1)}, bf16[1,8,48,4096]{3,2,1,0:T(8,128)(2,1)}, u32[]{:S(2)}) %copy-start) | copy-done | bytes 3145752
  11.3 0.0 copy-start.2
  11.3 0.7 copy-done.2
  12.0 8.2 %shard_map.104.ext_ref = bf16[33,48,512]{2,1,0:T(8,128)(2,1)S(1)} custom-call(s32[8]{0:T(128)S(1)} %bitcast.7, bf16[8,48,4096]{2,1,0:T(8,128)(2,1)S(1)} %bitcast.6, bf16[4096,32]{1,0:T(8,128)(2,1)S(1)} %copy.13.occ_ref, s32[1,256]{1,0:T(1,128)S(1)} %broadcast_in_dim_tile.3.order_ref, f32[8,256]{1,0:T(8,128)S(1)} %reshape.97.merge_ref), custom_call_target="tpu_custom_call" | custom-call | tf_op jit(solution)/shard_map/pallas_call | solution.py:80
  20.1 0.0 copy-start.1
  20.2 1.2 copy-done.1
  21.3 7.2 %copy.14.vir_ref = bf16[1408,1600]{1,0:T(8,128)(2,1)} copy(bf16[1408,1600]{0,1:T(8,128)(2,1)} %param.14) | data formatting | bytes 9011200 | tf_op args[5]
  28.5 134.6 %shard_map.105 = (bf16[1,200,1600]{2,1,0:T(8,128)(2,1)}, f32[1]{0:T(128)}) custom-call(bf16[33,48,512]{2,1,0:T(8,128)(2,1)} %copy-done.1, s32[8,128]{1,0:T(8,128)} %broadcast_in_dim.30.meta_ref, bf16[1408,1600]{1,0:T(8,128)(2,1)} %copy.14.vir_ref, f32[1,1600]{1,0:T(1,128)} %broadcast_in_dim.48.erow_ref, f32[8,1,256]{2,1,0:T(1,128)} %pad.4.eblock_ref, ...), custom_call_target="tpu_custom_call" | custom-call | flops 14394851328 | bytes 4505600 | tf_op jit(solution)/shard_map/pallas_call | solution.py:433
  163.1 2.0 %copy.18 = bf16[1,200,1600]{2,1,0:T(8,128)(2,1)} copy(bf16[1,200,1600]{2,1,0:T(8,128)(2,1)} %get-tuple-element.6) | data formatting | bytes 1280000
  (5 shorter events, 0.0 us)
Async XLA Ops:
  9.4 1.9 %copy-start = (bf16[1,8,48,4096]{3,2,1,0:T(8,128)(2,1)S(1)}, bf16[1,8,48,4096]{3,2,1,0:T(8,128)(2,1)}, u32[]{:S(2)}) copy-start(bf16[1,8,48,4096]{3,2,1,0:T(8,128)(2,1)} %param.9) | copy-start | bytes 9437188
  11.3 0.7 copy-start.2
  20.1 1.2 copy-start.1

commit v2 on v1

v2 whole, which is shorter than its diff:
```python
import functools

import jax
import jax.numpy as jnp
from jax import lax
from jax.experimental import pallas as pl
from jax.experimental.pallas import tpu as pltpu
from jax.sharding import PartitionSpec as P

SHELL = 64
LANE = 128
ROWS = 16
HALF = ROWS // 2
MESH = pl.DeviceIdType.MESH
F32 = jnp.float32
BF16 = jnp.bfloat16
I32 = jnp.int32
NT = (((1,), (1,)), ((), ()))


def left_half(shape):
    return lax.broadcasted_iota(I32, shape, len(shape) - 1) < SHELL


def iota(shape, dim):
    return lax.broadcasted_iota(I32, shape, dim)


def first_of_kind(slots, nu_ref, count):
    live = [k < count for k in range(slots)]
    first = []
    for k in range(slots):
        new = live[k]
        for j in range(k):
            new = new & (nu_ref[0, j] != nu_ref[0, k])
        first.append(new)
    return live, first


def build_mixer(slots, occ_count, mu_ref, nu_ref, order_ref, live, first, occ, tall, mixer):
    lane_tiles = SHELL * SHELL // LANE
    depth = slots * lane_tiles
    wide = slots * occ_count
    lane = iota((1, wide), 1)
    batch = lane % occ_count
    target = lane // occ_count
    order = jnp.zeros((1, wide), I32)
    for i in range(occ_count):
        order = jnp.where(batch == i, order_ref[i], order)
    shell = jnp.full((1, wide), -1, I32)
    for k in range(slots):
        shell = jnp.where(target == k, jnp.where(first[k], nu_ref[0, k], -1), shell)
    picked = iota((occ_count, wide), 0) == order
    row = iota((SHELL, LANE), 0)
    col = iota((SHELL, LANE), 1)
    wanted = 2 * (row % lane_tiles) + row // lane_tiles
    for k in range(slots):
        mu = mu_ref[0, k]
        rows = occ[:, :LANE]
        for t in range(1, occ.shape[1] // LANE):
            rows = jnp.where(mu // 2 == t, occ[:, t * LANE : (t + 1) * LANE], rows)
        split = (col == wanted + mu % 2 * SHELL).astype(F32).astype(BF16)
        parted = lax.dot_general(split, rows, NT, preferred_element_type=F32).astype(BF16)
        here = jnp.where(live[k], nu_ref[0, k], -2)
        picker = (picked & (shell == here)).astype(F32).astype(BF16)
        both = jnp.dot(parted, picker, preferred_element_type=F32)
        tall[k * lane_tiles : (k + 1) * lane_tiles, :] = both[:lane_tiles]
        tall[depth + k * lane_tiles : depth + (k + 1) * lane_tiles, :] = both[lane_tiles:]
    mixer[...] = tall[...].T.astype(BF16)


def place_table(slots, nu_ref, first):
    shell = iota((8, LANE), 1)
    place = jnp.full((8, LANE), slots, I32)
    for k in range(slots):
        here = jnp.where(first[k], nu_ref[0, k], -1)
        turned = jnp.where(shell % 2 == k % 2, k // 2, slots // 2 + k // 2)
        place = jnp.where(shell == here, turned, place)
    return place


def half_transform(slots, occ_count, q, blocks, mixer, spread, prods, ext):
    lane_tiles = SHELL * SHELL // LANE
    depth = slots * lane_tiles
    wide = slots * occ_count

    @pl.loop(0, slots)
    def _(k):
        for t in range(lane_tiles):
            at = pl.multiple_of((k * lane_tiles + t) * ROWS, ROWS)
            spread[pl.ds(at, ROWS), :] = blocks[q, k, :, t * LANE : (t + 1) * LANE].astype(F32)

    left = left_half((depth, LANE))
    for r in range(0, HALF, 2):
        columns = []
        for e in range(2):
            one = spread[pl.ds(r + e, depth, stride=ROWS), :]
            two = spread[pl.ds(r + e + HALF, depth, stride=ROWS), :]
            low = jnp.where(left, one, pltpu.roll(two, SHELL, 1))
            high = jnp.where(left, pltpu.roll(one, SHELL, 1), two)
            columns.append(jnp.concatenate([low, high], axis=0).astype(BF16))
        both = jnp.dot(mixer[...], jnp.concatenate(columns, axis=1), preferred_element_type=F32)
        for e in range(2):
            prods[(r + e) * wide : (r + e + 1) * wide, :] = both[:, e * LANE : (e + 1) * LANE]

    left = left_half((HALF, LANE))
    for i in range(occ_count + 1):
        batch = (i - 1) % occ_count
        for s in range(slots // 2):
            one = prods[pl.ds(2 * s * occ_count + batch, HALF, stride=wide), :]
            two = prods[pl.ds((2 * s + 1) * occ_count + batch, HALF, stride=wide), :]
            top = jnp.where(left, one, pltpu.roll(two, SHELL, 1))
            low = jnp.where(left, pltpu.roll(one, SHELL, 1), two)
            ext[q, i, :, s * LANE : (s + 1) * LANE] = jnp.concatenate([top, low], axis=0).astype(BF16)


def folded(values):
    rows, cols = values.shape
    if cols % LANE:
        values = jnp.concatenate([values, jnp.zeros((rows, LANE - cols % LANE), F32)], axis=1)
    result = values[:, :LANE]
    for c in range(LANE, values.shape[1], LANE):
        result = result + values[:, c : c + LANE]
    return jnp.sum(result.reshape(rows // 8, 8, LANE), axis=0)


def pair_kernel(
    n_aux,
    n_occ,
    pieces,
    integrals_ref,
    mu_ref,
    nu_ref,
    count_ref,
    occ_ref,
    vir_ref,
    order_ref,
    eocc_ref,
    evir_ref,
    amp_ref,
    energy_ref,
    blocks,
    occ,
    tall,
    mixer,
    spread,
    prods,
    ext,
    got,
    meta,
    metas,
    places,
    tiles,
    half_y,
    half_x,
    vir,
    vir_t,
    erow,
    eblock,
    lhs,
    wide,
    own,
    out_ring,
    in_ring,
    out_tile,
    in_tile,
    ratios,
    part,
    parts,
    local_sem,
    keep_sem,
    meta_send,
    meta_recv,
    data_send,
    data_recv,
    pass_send,
    pass_recv,
    ring_send,
    ring_recv,
    tile_send,
    tile_recv,
    part_send,
    part_recv,
):
    a = lax.axis_index("aux")
    g = lax.axis_index("occ")
    odd = lax.rem(a, 2)
    chip = a // 2
    mate = a + 1 - 2 * odd
    chips = n_aux // 2
    slots = blocks.shape[1]
    chunks = blocks.shape[0]
    occ_count = occ.shape[0]
    nvir, nu_w = vir.shape
    width = nvir // n_occ
    padded = vir_t.shape[1]
    slab = chunks * ROWS
    packs = slots // 2
    nu_tiles = nu_w // LANE

    def near(step):
        if chips != 16:
            return lax.rem(chip + step + chips, chips)
        return lax.rem(chip // 4 + step // 4, 4) * 4 + lax.rem(chip + step, 4)

    def back(step):
        if chips != 16:
            return lax.rem(chip - step + chips, chips)
        return lax.rem(chip // 4 - step // 4 + 4, 4) * 4 + lax.rem(chip % 4 - step % 4 + 4, 4)

    def around(step):
        return lax.rem(g + step + 2 * n_occ, n_occ)

    loads = [pltpu.make_async_copy(occ_ref, occ, local_sem.at[0])]
    for q in range(chunks):
        loads.append(
            pltpu.make_async_copy(integrals_ref.at[:, pl.ds(q * ROWS, ROWS)], blocks.at[q], local_sem.at[q + 1])
        )
    load_vir = pltpu.make_async_copy(vir_ref, vir, local_sem.at[chunks + 1])
    for load in loads:
        load.start()
    load_vir.start()

    barrier = pltpu.get_barrier_semaphore()

    @pl.loop(1, chips)
    def _(d):
        pl.semaphore_signal(barrier, inc=1, device_id={"aux": 2 * near(d) + odd}, device_id_type=MESH)

    pl.semaphore_signal(barrier, inc=1, device_id={"aux": mate}, device_id_type=MESH)

    @pl.loop(1, n_occ)
    def _(d):
        pl.semaphore_signal(barrier, inc=1, device_id={"occ": around(d)}, device_id_type=MESH)

    live, first = first_of_kind(slots, nu_ref, count_ref[0])
    meta[...] = place_table(slots, nu_ref, first)
    metas[odd, chip] = meta[...]
    loads[0].wait()
    build_mixer(slots, occ_count, mu_ref, nu_ref, order_ref, live, first, occ, tall, mixer)

    def meta_copy(d):
        return pltpu.make_async_remote_copy(
            meta,
            metas.at[odd, chip],
            meta_send.at[d],
            meta_recv.at[d],
            device_id={"aux": 2 * near(d) + odd},
            device_id_type=MESH,
        )

    def meta_pass():
        return pltpu.make_async_remote_copy(
            metas.at[odd], metas.at[odd], meta_send.at[0], meta_recv.at[0], device_id={"aux": mate}, device_id_type=MESH
        )

    def data_copy(q, d):
        to = near(d)
        return pltpu.make_async_remote_copy(
            ext.at[q, pl.ds(2 * to, 3)],
            got.at[odd, chip, q],
            data_send.at[q, d],
            data_recv.at[q, d],
            device_id={"aux": 2 * to + odd},
            device_id_type=MESH,
        )

    def keep_copy(q):
        return pltpu.make_async_copy(ext.at[q, pl.ds(2 * chip, 3)], got.at[odd, chip, q], keep_sem.at[q])

    def pass_copy(q, d):
        view = got.at[odd, back(d), q, pl.ds(1 - odd, 2)]
        return pltpu.make_async_remote_copy(
            view, view, pass_send.at[q, d], pass_recv.at[q, d], device_id={"aux": mate}, device_id_type=MESH
        )

    pl.semaphore_wait(barrier, chips + n_occ - 1)

    @pl.loop(1, chips)
    def _(d):
        meta_copy(d).start()

    @pl.loop(0, chunks)
    def _(q):
        pltpu.make_async_copy(
            integrals_ref.at[:, pl.ds(pl.multiple_of(q * ROWS, ROWS), ROWS)], blocks.at[q], local_sem.at[q + 1]
        ).wait()
        half_transform(slots, occ_count, q, blocks, mixer, spread, prods, ext)
        keep_copy(q).start()

        @pl.loop(1, chips)
        def _(d):
            data_copy(q, d).start()

    tiles[:, 2 * packs] = jnp.zeros((2, slab, LANE), BF16)
    load_vir.wait()
    for c in range(n_occ):
        low = c * width // ROWS * ROWS
        high = -(-(c + 1) * width // ROWS) * ROWS
        off = c * width - low
        for w in range(0, nu_w, LANE):
            rows = vir[low:high, w : w + LANE].astype(F32)[off : off + width]
            if padded > width:
                rows = jnp.concatenate([rows, jnp.zeros((padded - width, LANE), F32)], axis=0)
            vir_t[c, :, w : w + LANE] = rows.astype(BF16)
    erow[...] = evir_ref[...].reshape(1, nvir)
    for c in range(n_occ):
        eblock[c] = jnp.concatenate(
            [erow[:, c * width : (c + 1) * width], jnp.ones((1, eblock.shape[2] - width), F32)], axis=1
        )

    @pl.loop(1, chips)
    def _(d):
        meta_copy(d).wait_recv()

    meta_pass().start()
    meta_pass().wait_recv()
    placing = pltpu.make_async_copy(metas, places, local_sem.at[chunks + 2])
    placing.start()

    for q in range(chunks):
        keep_copy(q).wait()
        pass_copy(q, 0).start()
    placing.wait()

    left = left_half((slab, LANE))

    def spread_out(parity, source):
        for side in range(2):
            for s in range(packs):
                tile = got[parity, source, :, odd + side, :, s * LANE : (s + 1) * LANE].reshape(slab, LANE)
                tiles[side, s] = tile
                tiles[side, packs + s] = pltpu.roll(tile.astype(F32), SHELL, 1).astype(BF16)
        rows = pl.ds(pl.multiple_of((parity * chips + source) * slab, ROWS), slab)
        for c in range(nu_tiles):
            one = places[parity, source, 0, 2 * c]
            two = places[parity, source, 0, 2 * c + 1]
            columns = slice(c * LANE, (c + 1) * LANE)
            half_y[rows, columns] = jnp.where(left, tiles[0, one], tiles[0, two])
            half_x[rows, columns] = jnp.where(left, tiles[1, one], tiles[1, two])

    spread_out(odd, chip)

    @pl.loop(0, chunks)
    def _(q):
        @pl.loop(1, chips)
        def _(d):
            data_copy(q, d).wait_recv()
            pass_copy(q, d).start()

            @pl.when(q == chunks - 1)
            def _():
                spread_out(odd, back(d))

    @pl.loop(0, chips)
    def _(d):
        @pl.loop(0, chunks)
        def _(q):
            pass_copy(q, d).wait_recv()

        spread_out(1 - odd, back(d))

    way = 1 - 2 * odd

    def ring_copy(t, k):
        row, rows, sign = pieces[k]
        return pltpu.make_async_remote_copy(
            out_ring.at[t, pl.ds(row, rows)],
            in_ring.at[t, pl.ds(row, rows)],
            ring_send.at[k, t],
            ring_recv.at[k, t],
            device_id={"occ": around(way * sign)},
            device_id_type=MESH,
        )

    @pl.loop(0, n_occ)
    def _(t):
        for row, rows, sign in pieces:
            lhs[row : row + rows, :] = vir_t[around(-sign * way * (t + 1)), row : row + rows, :]
        for p in range(0, n_aux * slab, 256):
            end = min(p + 256, n_aux * slab)
            wide[:, p:end] = lax.dot_general(lhs[...], half_y[p:end, :], NT, preferred_element_type=F32).astype(BF16)
        for c in range(0, nu_w, 256):
            end = min(c + 256, nu_w)
            own[:, c:end] = jnp.dot(wide[...], half_x[:, c:end], preferred_element_type=F32)
        for k, (row, rows, sign) in enumerate(pieces):
            span = slice(row, row + rows)

            @pl.when(t == 0)
            def _():
                out_ring[t, span, :] = own[span, :].astype(BF16)

            @pl.when(t > 0)
            def _():
                ring_copy(t - 1, k).wait_recv()
                out_ring[t, span, :] = (own[span, :] + in_ring[t - 1, span, :].astype(F32)).astype(BF16)

            @pl.when(t < n_occ - 1)
            def _():
                ring_copy(t, k).start()

    last = n_occ - 1
    farthest = n_occ // 2

    def tile_step(d):
        return way * (d if d % 2 == 1 else -d)

    def tile_copy(d):
        return pltpu.make_async_remote_copy(
            out_tile.at[d - 1],
            in_tile.at[d - 1],
            tile_send.at[d - 1],
            tile_recv.at[d - 1],
            device_id={"occ": around(tile_step(d))},
            device_id_type=MESH,
        )

    for d in range(farthest, 0, -1):
        out_tile[d - 1] = lax.dot_general(
            vir_t[around(tile_step(d))], out_ring[last], NT, preferred_element_type=F32
        ).astype(BF16)
        tile_copy(d).start()

    e_pair = eocc_ref[order_ref[a]] + eocc_ref[order_ref[lax.rem(a + n_aux - 1, n_aux)]]
    block_row = jnp.broadcast_to(eblock[g], (8, eblock.shape[2]))
    e_rows = e_pair - block_row.T[:padded, 0:1]

    total = jnp.zeros((8, LANE), F32)
    for c in range(0, nvir, 256):
        end = min(c + 256, nvir)
        pair = lax.dot_general(out_ring[last], vir[c:end, :], NT, preferred_element_type=F32)
        ratio = pair / (e_rows - erow[:, c:end])
        amp_ref[0, :, c:end] = ratio[:width].astype(BF16)
        total = total + folded(ratio * (2.0 * pair))

    def block_ratio(h):
        block = lax.dot_general(out_ring[last], vir_t[h], NT, preferred_element_type=F32)
        return block / (e_rows - eblock[h][:, :padded])

    same = lax.dot_general(vir_t[g], out_ring[last], NT, preferred_element_type=F32)
    total = total - folded(block_ratio(g) * same)
    for d in range(1, farthest + 1):
        ratios[d - 1] = block_ratio(around(-tile_step(d)))
    for d in range(1, farthest + 1):
        weight = 1.0 if 2 * d == n_occ else 2.0
        tile_copy(d).wait_recv()
        total = total - weight * folded(ratios[d - 1] * in_tile[d - 1].astype(F32))

    part[...] = total

    def part_copy(d):
        return pltpu.make_async_remote_copy(
            part, parts.at[d], part_send.at[d], part_recv.at[d], device_id={"occ": around(d)}, device_id_type=MESH
        )

    for d in range(1, n_occ):
        part_copy(d).start()
    for d in range(1, n_occ):
        part_copy(d).wait_recv()
        total = total + parts[d]
    energy_ref[0] = jnp.sum(total) / (nvir * nvir)

    for d in range(1, n_occ):
        part_copy(d).wait_send()
    for d in range(1, farthest + 1):
        tile_copy(d).wait_send()

    @pl.loop(0, n_occ - 1)
    def _(t):
        for k in range(len(pieces)):
            ring_copy(t, k).wait_send()

    meta_pass().wait_send()

    @pl.loop(1, chips)
    def _(d):
        meta_copy(d).wait_send()

    @pl.loop(0, chunks)
    def _(q):
        pass_copy(q, 0).wait_send()

        @pl.loop(1, chips)
        def _(d):
            data_copy(q, d).wait_send()
            pass_copy(q, d).wait_send()


def pair_results(
    n_aux, n_occ, integrals, mu_shells, nu_shells, block_count, occ_t, vir_t, occ_order, occ_energies, vir_energies
):
    slots, slab, _ = integrals.shape
    occ_count, nao = occ_t.shape
    nvir, nu_w = vir_t.shape
    width = nvir // n_occ
    padded = -(-width // ROWS) * ROWS
    chunks = slab // ROWS
    chips = n_aux // 2
    aux_rows = n_aux * slab
    farthest = n_occ // 2
    spread_rows = slots * SHELL * SHELL // LANE * ROWS
    mixed = slots * occ_count
    cuts = [padded * k // (4 * ROWS) * ROWS for k in range(5)]
    spans = [(low, high - low, sign) for low, high, sign in zip(cuts[:-1], cuts[1:], (1, 1, -1, -1))]
    pieces = [spans[k] for k in (0, 2, 1, 3) if spans[k][1]]
    vmem = pl.BlockSpec(memory_space=pltpu.VMEM)
    smem = pl.BlockSpec(memory_space=pltpu.SMEM)
    anywhere = pl.BlockSpec(memory_space=pl.ANY)
    dma = pltpu.SemaphoreType.DMA
    macs = 2 * n_occ * padded * aux_rows * nu_w
    return pl.pallas_call(
        functools.partial(pair_kernel, n_aux, n_occ, pieces),
        in_specs=[anywhere, smem, smem, smem, anywhere, anywhere, smem, smem, vmem],
        out_specs=(vmem, smem),
        out_shape=(jax.ShapeDtypeStruct((1, width, nvir), BF16), jax.ShapeDtypeStruct((1,), F32)),
        scratch_shapes=[
            pltpu.VMEM((chunks, slots, ROWS, SHELL * SHELL), BF16),
            pltpu.VMEM((occ_count, nao), BF16),
            pltpu.VMEM((slots * SHELL, mixed), F32),
            pltpu.VMEM((mixed, slots * SHELL), BF16),
            pltpu.VMEM((spread_rows, LANE), F32),
            pltpu.VMEM((HALF * mixed, LANE), F32),
            pltpu.VMEM((chunks, occ_count + 1, ROWS, slots * SHELL), BF16),
            pltpu.VMEM((2, chips, chunks, 3, ROWS, slots * SHELL), BF16),
            pltpu.VMEM((8, LANE), I32),
            pltpu.VMEM((2, chips, 8, LANE), I32),
            pltpu.SMEM((2, chips, 8, LANE), I32),
            pltpu.VMEM((2, slots + 1, slab, LANE), BF16),
            pltpu.VMEM((aux_rows, nu_w), BF16),
            pltpu.VMEM((aux_rows, nu_w), BF16),
            pltpu.VMEM((nvir, nu_w), BF16),
            pltpu.VMEM((n_occ, padded, nu_w), BF16),
            pltpu.VMEM((1, nvir), F32),
            pltpu.VMEM((n_occ, 1, -(-padded // LANE) * LANE), F32),
            pltpu.VMEM((padded, nu_w), BF16),
            pltpu.VMEM((padded, aux_rows), BF16),
            pltpu.VMEM((padded, nu_w), F32),
            pltpu.VMEM((n_occ, padded, nu_w), BF16),
            pltpu.VMEM((n_occ - 1, padded, nu_w), BF16),
            pltpu.VMEM((farthest, padded, padded), BF16),
            pltpu.VMEM((farthest, padded, padded), BF16),
            pltpu.VMEM((farthest, padded, padded), F32),
            pltpu.VMEM((8, LANE), F32),
            pltpu.VMEM((n_occ, 8, LANE), F32),
            dma((chunks + 3,)),
            dma((chunks,)),
            dma((chips,)),
            dma((chips,)),
            dma((chunks, chips)),
            dma((chunks, chips)),
            dma((chunks, chips)),
            dma((chunks, chips)),
            dma((len(pieces), n_occ - 1)),
            dma((len(pieces), n_occ - 1)),
            dma((farthest,)),
            dma((farthest,)),
            dma((n_occ,)),
            dma((n_occ,)),
        ],
        compiler_params=pltpu.CompilerParams(
            collective_id=0, has_side_effects=True, vmem_limit_bytes=60 * 2**20
        ),
        cost_estimate=pl.CostEstimate(flops=2 * macs, bytes_accessed=2 * nu_w * nvir, transcendentals=0),
    )(integrals, mu_shells, nu_shells, block_count, occ_t, vir_t, occ_order, occ_energies, vir_energies)


def local(
    n_aux,
    n_occ,
    integrals,
    mu_shells,
    nu_shells,
    block_count,
    occ_coeffs,
    vir_coeffs,
    occ_order,
    occ_energies,
    vir_energies,
):
    return pair_results(
        n_aux,
        n_occ,
        integrals[0],
        mu_shells,
        nu_shells,
        block_count,
        occ_coeffs.T,
        vir_coeffs.T,
        occ_order,
        occ_energies,
        vir_energies,
    )


def solution(mesh):
    placed = (
        P(("aux", "occ"), None, None, None),
        P(("aux", "occ"), None),
        P(("aux", "occ"), None),
        P(("aux", "occ")),
        P(),
        P(),
        P(),
        P(),
        P(),
    )
    return jax.shard_map(
        functools.partial(local, mesh.shape["aux"], mesh.shape["occ"]),
        mesh=mesh,
        in_specs=placed,
        out_specs=(P("aux", "occ", None), P("aux")),
        check_vma=False,
    )
```

time: 167 us -> 122 us (0.73)
  the two profiles are of different devices: /device:TPU:1 before, /device:TPU:30 now
where the time goes in v2:
time: 122 us
  Pallas kernels  117 us (96%)
  between operations  3.05 us (2%)
  local copies, waits for them, and re-layouts  1.98 us (2%)
    pallas_call x1, Pallas kernels, pair_results(): pl.pallas_call(functools.partial(pair_kernel, n_aux, n_occ, pieces), in_s...  117 us

profile of v2, /device:TPU:30, one launch (start us, length us, event | category | flops | bytes accessed | tf_op | source)
XLA Modules:
  0.0 122.0 jit_solution(6868220265826954252)
XLA Ops:
  1.3 117.0 %shard_map.104 = (bf16[1,200,1600]{2,1,0:T(8,128)(2,1)}, f32[1]{0:T(128)}) custom-call(bf16[8,48,4096]{2,1,0:T(8,128)(2,1)} %bitcast.4, s32[1,8]{1,0:T(1,128)} %mu_ref.1, s32[1,8]{1,0:T(1,128)} %nu_ref.1, s32[1]{0:T(128)S(6)} %copy.13.count_ref, bf16[32,4096]{1,0:T(8,128)(2,1)} %bitcast.5, bf16[1600,1408]{1,0:T(8,128)(2,1)} %bitcast.3, s32[32]{0:T(128)} %order_ref.1, ...), custom_call_target="tpu_custom_call" | custom-call | flops 14394851328 | bytes 4505600 | tf_op jit(solution)/shard_map/pallas_call | solution.py:511
  118.3 2.0 %copy.14 = bf16[1,200,1600]{2,1,0:T(8,128)(2,1)} copy(bf16[1,200,1600]{2,1,0:T(8,128)(2,1)} %get-tuple-element.4) | data formatting | bytes 1280000

commit v3 on v2

--- a/solution.py
+++ b/solution.py
@@ -24,6 +24,11 @@
 
 def iota(shape, dim):
     return lax.broadcasted_iota(I32, shape, dim)
+
+
+def halves_apart(one, two, left):
+    turned = pltpu.roll(jnp.where(left, two, one), SHELL, 1)
+    return [jnp.where(left, one, turned), jnp.where(left, turned, two)]
 
 
 def first_of_kind(slots, nu_ref, count):
@@ -96,9 +101,7 @@
         for e in range(2):
             one = spread[pl.ds(r + e, depth, stride=ROWS), :]
             two = spread[pl.ds(r + e + HALF, depth, stride=ROWS), :]
-            low = jnp.where(left, one, pltpu.roll(two, SHELL, 1))
-            high = jnp.where(left, pltpu.roll(one, SHELL, 1), two)
-            columns.append(jnp.concatenate([low, high], axis=0).astype(BF16))
+            columns.append(jnp.concatenate(halves_apart(one, two, left), axis=0).astype(BF16))
         both = jnp.dot(mixer[...], jnp.concatenate(columns, axis=1), preferred_element_type=F32)
         for e in range(2):
             prods[(r + e) * wide : (r + e + 1) * wide, :] = both[:, e * LANE : (e + 1) * LANE]
@@ -109,9 +112,8 @@
         for s in range(slots // 2):
             one = prods[pl.ds(2 * s * occ_count + batch, HALF, stride=wide), :]
             two = prods[pl.ds((2 * s + 1) * occ_count + batch, HALF, stride=wide), :]
-            top = jnp.where(left, one, pltpu.roll(two, SHELL, 1))
-            low = jnp.where(left, pltpu.roll(one, SHELL, 1), two)
-            ext[q, i, :, s * LANE : (s + 1) * LANE] = jnp.concatenate([top, low], axis=0).astype(BF16)
+            pair = jnp.concatenate(halves_apart(one, two, left), axis=0)
+            ext[q, i, :, s * LANE : (s + 1) * LANE] = pair.astype(BF16)
 
 
 def folded(values):
@@ -162,9 +164,15 @@
     own,
     out_ring,
     in_ring,
-    out_tile,
-    in_tile,
-    ratios,
+    out_rest,
+    in_rest,
+    total_u,
+    out_lead,
+    in_lead,
+    out_tail,
+    in_tail,
+    ratio_lead,
+    ratio_tail,
     part,
     parts,
     local_sem,
@@ -177,8 +185,10 @@
     pass_recv,
     ring_send,
     ring_recv,
-    tile_send,
-    tile_recv,
+    lead_send,
+    lead_recv,
+    tail_send,
+    tail_recv,
     part_send,
     part_recv,
 ):
@@ -292,7 +302,7 @@
         def _(d):
             data_copy(q, d).start()
 
-    tiles[:, 2 * packs] = jnp.zeros((2, slab, LANE), BF16)
+    tiles[:, 2 * packs] = jnp.zeros((2, ROWS, LANE), BF16)
     load_vir.wait()
     for c in range(n_occ):
         low = c * width // ROWS * ROWS
@@ -323,15 +333,16 @@
         pass_copy(q, 0).start()
     placing.wait()
 
-    left = left_half((slab, LANE))
-
-    def spread_out(parity, source):
+    left = left_half((ROWS, LANE))
+    batch_rows = n_aux * ROWS
+
+    def spread_out(q, parity, source):
         for side in range(2):
             for s in range(packs):
-                tile = got[parity, source, :, odd + side, :, s * LANE : (s + 1) * LANE].reshape(slab, LANE)
+                tile = got[parity, source, q, odd + side, :, s * LANE : (s + 1) * LANE]
                 tiles[side, s] = tile
                 tiles[side, packs + s] = pltpu.roll(tile.astype(F32), SHELL, 1).astype(BF16)
-        rows = pl.ds(pl.multiple_of((parity * chips + source) * slab, ROWS), slab)
+        rows = pl.ds(pl.multiple_of(q * batch_rows + (parity * chips + source) * ROWS, ROWS), ROWS)
         for c in range(nu_tiles):
             one = places[parity, source, 0, 2 * c]
             two = places[parity, source, 0, 2 * c + 1]
@@ -339,121 +350,226 @@
             half_y[rows, columns] = jnp.where(left, tiles[0, one], tiles[0, two])
             half_x[rows, columns] = jnp.where(left, tiles[1, one], tiles[1, two])
 
-    spread_out(odd, chip)
+    way = 1 - 2 * odd
+    whole = out_ring.shape[1]
+    front = out_rest.shape[2]
+    rest = (whole, padded - whole, 1)
+
+    def pick_rows(t):
+        for row, rows, sign in pieces + [rest]:
+            lhs[row : row + rows, :] = vir_t[around(-sign * way * (t + 1)), row : row + rows, :]
+
+    def column_cuts(step):
+        return [(c, min(c + step, nu_w)) for c in range(0, nu_w, step)]
+
+    pick_rows(0)
 
     @pl.loop(0, chunks)
     def _(q):
+        spread_out(q, odd, chip)
+
         @pl.loop(1, chips)
         def _(d):
             data_copy(q, d).wait_recv()
             pass_copy(q, d).start()
-
-            @pl.when(q == chunks - 1)
-            def _():
-                spread_out(odd, back(d))
-
-    @pl.loop(0, chips)
-    def _(d):
-        @pl.loop(0, chunks)
-        def _(q):
+            spread_out(q, odd, back(d))
+
+        @pl.loop(0, chips)
+        def _(d):
             pass_copy(q, d).wait_recv()
-
-        spread_out(1 - odd, back(d))
-
-    way = 1 - 2 * odd
+            spread_out(q, 1 - odd, back(d))
+
+        rows = pl.ds(pl.multiple_of(q * batch_rows, ROWS), batch_rows)
+        wide[:, :batch_rows] = lax.dot_general(
+            lhs[...], half_y[rows, :], NT, preferred_element_type=F32
+        ).astype(BF16)
+
+        @pl.when(q == 0)
+        def _():
+            for low, high in column_cuts(256):
+                own[:, low:high] = jnp.dot(wide[:, :batch_rows], half_x[rows, low:high], preferred_element_type=F32)
+
+        @pl.when(q > 0)
+        def _():
+            for low, high in column_cuts(256):
+                own[:, low:high] += jnp.dot(wide[:, :batch_rows], half_x[rows, low:high], preferred_element_type=F32)
 
     def ring_copy(t, k):
-        row, rows, sign = pieces[k]
+        if k == len(pieces):
+            source, target = out_rest.at[t], in_rest.at[t]
+            sign = 1
+        else:
+            row, rows, sign = pieces[k]
+            source, target = out_ring.at[t, pl.ds(row, rows)], in_ring.at[t, pl.ds(row, rows)]
         return pltpu.make_async_remote_copy(
-            out_ring.at[t, pl.ds(row, rows)],
-            in_ring.at[t, pl.ds(row, rows)],
+            source,
+            target,
             ring_send.at[k, t],
             ring_recv.at[k, t],
             device_id={"occ": around(way * sign)},
             device_id_type=MESH,
         )
 
+    def packed_rest():
+        back_part = own[whole : whole + 8, front:]
+        if back_part.shape[1] < front:
+            back_part = jnp.concatenate([back_part, jnp.zeros((8, front - back_part.shape[1]), F32)], axis=1)
+        return jnp.concatenate([own[whole : whole + 8, :front], back_part], axis=0)
+
     @pl.loop(0, n_occ)
     def _(t):
-        for row, rows, sign in pieces:
-            lhs[row : row + rows, :] = vir_t[around(-sign * way * (t + 1)), row : row + rows, :]
-        for p in range(0, n_aux * slab, 256):
-            end = min(p + 256, n_aux * slab)
-            wide[:, p:end] = lax.dot_general(lhs[...], half_y[p:end, :], NT, preferred_element_type=F32).astype(BF16)
-        for c in range(0, nu_w, 256):
-            end = min(c + 256, nu_w)
-            own[:, c:end] = jnp.dot(wide[...], half_x[:, c:end], preferred_element_type=F32)
-        for k, (row, rows, sign) in enumerate(pieces):
-            span = slice(row, row + rows)
+        @pl.when(t > 0)
+        def _():
+            pick_rows(t)
+            for p in range(0, n_aux * slab, 256):
+                end = min(p + 256, n_aux * slab)
+                wide[:, p:end] = lax.dot_general(
+                    lhs[...], half_y[p:end, :], NT, preferred_element_type=F32
+                ).astype(BF16)
+            for low, high in column_cuts(256):
+                own[:, low:high] = jnp.dot(wide[...], half_x[:, low:high], preferred_element_type=F32)
+
+        for k in range(len(pieces) + 1):
+            if k < len(pieces):
+                span = slice(pieces[k][0], pieces[k][0] + pieces[k][1])
 
             @pl.when(t == 0)
             def _():
-                out_ring[t, span, :] = own[span, :].astype(BF16)
+                if k < len(pieces):
+                    out_ring[t, span, :] = own[span, :].astype(BF16)
+                else:
+                    out_rest[t] = packed_rest().astype(BF16)
 
             @pl.when(t > 0)
             def _():
                 ring_copy(t - 1, k).wait_recv()
-                out_ring[t, span, :] = (own[span, :] + in_ring[t - 1, span, :].astype(F32)).astype(BF16)
+                if k < len(pieces):
+                    out_ring[t, span, :] = (own[span, :] + in_ring[t - 1, span, :].astype(F32)).astype(BF16)
+                else:
+                    out_rest[t] = (packed_rest() + in_rest[t - 1].astype(F32)).astype(BF16)
 
             @pl.when(t < n_occ - 1)
             def _():
                 ring_copy(t, k).start()
 
     last = n_occ - 1
+    total_u[:whole, :] = out_ring[last]
+    packed = out_rest[last].astype(F32)
+    unpacked = jnp.concatenate([packed[:8], packed[8:, : nu_w - front]], axis=1)
+    total_u[whole:, :] = jnp.concatenate([unpacked, jnp.zeros((padded - whole - 8, nu_w), F32)], axis=0).astype(BF16)
+
     farthest = n_occ // 2
+    far = farthest - 1
+    far_block = around(farthest)
+    nearer_half = g < farthest
 
     def tile_step(d):
         return way * (d if d % 2 == 1 else -d)
 
-    def tile_copy(d):
+    def lead_copy(d):
         return pltpu.make_async_remote_copy(
-            out_tile.at[d - 1],
-            in_tile.at[d - 1],
-            tile_send.at[d - 1],
-            tile_recv.at[d - 1],
+            out_lead.at[d - 1],
+            in_lead.at[d - 1],
+            lead_send.at[d - 1],
+            lead_recv.at[d - 1],
             device_id={"occ": around(tile_step(d))},
             device_id_type=MESH,
         )
 
-    for d in range(farthest, 0, -1):
-        out_tile[d - 1] = lax.dot_general(
-            vir_t[around(tile_step(d))], out_ring[last], NT, preferred_element_type=F32
-        ).astype(BF16)
-        tile_copy(d).start()
+    def tail_copy(d):
+        return pltpu.make_async_remote_copy(
+            out_tail.at[d - 1],
+            in_tail.at[d - 1],
+            tail_send.at[d - 1],
+            tail_recv.at[d - 1],
+            device_id={"occ": around(tile_step(d))},
+            device_id_type=MESH,
+        )
+
+    def times(one, two):
+        return lax.dot_general(one, two, NT, preferred_element_type=F32)
+
+    @pl.when(nearer_half)
+    def _():
+        out_lead[far] = times(total_u[...], vir_t[far_block, :LANE, :]).astype(BF16)
+        lead_copy(farthest).start()
+
+    @pl.when(jnp.logical_not(nearer_half))
+    def _():
+        out_tail[far] = times(total_u[LANE:, :], vir_t[far_block]).astype(BF16)
+        tail_copy(farthest).start()
+
+    for d in range(far, 0, -1):
+        to = around(tile_step(d))
+        out_lead[d - 1] = times(total_u[...], vir_t[to, :LANE, :]).astype(BF16)
+        lead_copy(d).start()
+        out_tail[d - 1] = times(vir_t[to, LANE:, :], total_u[...]).astype(BF16)
+        tail_copy(d).start()
 
     e_pair = eocc_ref[order_ref[a]] + eocc_ref[order_ref[lax.rem(a + n_aux - 1, n_aux)]]
-    block_row = jnp.broadcast_to(eblock[g], (8, eblock.shape[2]))
-    e_rows = e_pair - block_row.T[:padded, 0:1]
-
+
+    def e_row(h, low, high):
+        return eblock[h][:, low:high]
+
+    def e_column(h, low, high):
+        return jnp.broadcast_to(eblock[h], (8, eblock.shape[2])).T[low:high, 0:1]
+
+    e_rows = e_pair - e_column(g, 0, padded)
     total = jnp.zeros((8, LANE), F32)
     for c in range(0, nvir, 256):
         end = min(c + 256, nvir)
-        pair = lax.dot_general(out_ring[last], vir[c:end, :], NT, preferred_element_type=F32)
+        pair = times(total_u[...], vir[c:end, :])
         ratio = pair / (e_rows - erow[:, c:end])
         amp_ref[0, :, c:end] = ratio[:width].astype(BF16)
         total = total + folded(ratio * (2.0 * pair))
 
-    def block_ratio(h):
-        block = lax.dot_general(out_ring[last], vir_t[h], NT, preferred_element_type=F32)
-        return block / (e_rows - eblock[h][:, :padded])
-
-    same = lax.dot_general(vir_t[g], out_ring[last], NT, preferred_element_type=F32)
-    total = total - folded(block_ratio(g) * same)
-    for d in range(1, farthest + 1):
-        ratios[d - 1] = block_ratio(around(-tile_step(d)))
-    for d in range(1, farthest + 1):
-        weight = 1.0 if 2 * d == n_occ else 2.0
-        tile_copy(d).wait_recv()
-        total = total - weight * folded(ratios[d - 1] * in_tile[d - 1].astype(F32))
+    block = times(total_u[...], vir_t[g])
+    same = times(vir_t[g], total_u[...])
+    total = total - folded(block / (e_rows - e_row(g, 0, padded)) * same)
+
+    def lead_ratio(h):
+        under = (e_pair - e_column(h, 0, padded)) - e_row(g, 0, LANE)
+        return times(vir_t[h], total_u[:LANE, :]) / under
+
+    for d in range(1, farthest):
+        source = around(-tile_step(d))
+        ratio_lead[d - 1] = lead_ratio(source)
+        ratio_tail[d - 1] = times(total_u[LANE:, :], vir_t[source]) / (e_rows[LANE:] - e_row(source, 0, padded))
+
+    @pl.when(nearer_half)
+    def _():
+        under = (e_pair - e_column(far_block, LANE, padded)) - e_row(g, 0, padded)
+        ratio_tail[far] = times(vir_t[far_block, LANE:, :], total_u[...]) / under
+
+    @pl.when(jnp.logical_not(nearer_half))
+    def _():
+        ratio_lead[far] = lead_ratio(far_block)
 
     part[...] = total
+    for d in range(1, farthest):
+        lead_copy(d).wait_recv()
+        tail_copy(d).wait_recv()
+        met = folded(ratio_lead[d - 1] * in_lead[d - 1].astype(F32))
+        part[...] -= 2.0 * (met + folded(ratio_tail[d - 1] * in_tail[d - 1].astype(F32)))
+
+    @pl.when(nearer_half)
+    def _():
+        tail_copy(farthest).wait_recv()
+        part[...] -= 2.0 * folded(ratio_tail[far] * in_tail[far].astype(F32))
+
+    @pl.when(jnp.logical_not(nearer_half))
+    def _():
+        lead_copy(farthest).wait_recv()
+        part[...] -= 2.0 * folded(ratio_lead[far] * in_lead[far].astype(F32))
+
+    total = part[...]
 
     def part_copy(d):
         return pltpu.make_async_remote_copy(
             part, parts.at[d], part_send.at[d], part_recv.at[d], device_id={"occ": around(d)}, device_id_type=MESH
         )
 
-    for d in range(1, n_occ):
+    for d in sorted(range(1, n_occ), key=lambda d: -min(d, n_occ - d)):
         part_copy(d).start()
     for d in range(1, n_occ):
         part_copy(d).wait_recv()
@@ -462,12 +578,21 @@
 
     for d in range(1, n_occ):
         part_copy(d).wait_send()
-    for d in range(1, farthest + 1):
-        tile_copy(d).wait_send()
+    for d in range(1, farthest):
+        lead_copy(d).wait_send()
+        tail_copy(d).wait_send()
+
+    @pl.when(nearer_half)
+    def _():
+        lead_copy(farthest).wait_send()
+
+    @pl.when(jnp.logical_not(nearer_half))
+    def _():
+        tail_copy(farthest).wait_send()
 
     @pl.loop(0, n_occ - 1)
     def _(t):
-        for k in range(len(pieces)):
+        for k in range(len(pieces) + 1):
             ring_copy(t, k).wait_send()
 
     meta_pass().wait_send()
@@ -500,7 +625,9 @@
     farthest = n_occ // 2
     spread_rows = slots * SHELL * SHELL // LANE * ROWS
     mixed = slots * occ_count
-    cuts = [padded * k // (4 * ROWS) * ROWS for k in range(5)]
+    whole = width // ROWS * ROWS
+    front = -(-nu_w // (2 * LANE)) * LANE
+    cuts = [whole * k // (4 * ROWS) * ROWS for k in range(5)]
     spans = [(low, high - low, sign) for low, high, sign in zip(cuts[:-1], cuts[1:], (1, 1, -1, -1))]
     pieces = [spans[k] for k in (0, 2, 1, 3) if spans[k][1]]
     vmem = pl.BlockSpec(memory_space=pltpu.VMEM)
@@ -525,7 +652,7 @@
             pltpu.VMEM((8, LANE), I32),
             pltpu.VMEM((2, chips, 8, LANE), I32),
             pltpu.SMEM((2, chips, 8, LANE), I32),
-            pltpu.VMEM((2, slots + 1, slab, LANE), BF16),
+            pltpu.VMEM((2, slots + 1, ROWS, LANE), BF16),
             pltpu.VMEM((aux_rows, nu_w), BF16),
             pltpu.VMEM((aux_rows, nu_w), BF16),
             pltpu.VMEM((nvir, nu_w), BF16),
@@ -535,11 +662,17 @@
             pltpu.VMEM((padded, nu_w), BF16),
             pltpu.VMEM((padded, aux_rows), BF16),
             pltpu.VMEM((padded, nu_w), F32),
-            pltpu.VMEM((n_occ, padded, nu_w), BF16),
-            pltpu.VMEM((n_occ - 1, padded, nu_w), BF16),
-            pltpu.VMEM((farthest, padded, padded), BF16),
-            pltpu.VMEM((farthest, padded, padded), BF16),
-            pltpu.VMEM((farthest, padded, padded), F32),
+            pltpu.VMEM((n_occ, whole, nu_w), BF16),
+            pltpu.VMEM((n_occ - 1, whole, nu_w), BF16),
+            pltpu.VMEM((n_occ, ROWS, front), BF16),
+            pltpu.VMEM((n_occ - 1, ROWS, front), BF16),
+            pltpu.VMEM((padded, nu_w), BF16),
+            pltpu.VMEM((farthest, padded, LANE), BF16),
+            pltpu.VMEM((farthest, padded, LANE), BF16),
+            pltpu.VMEM((farthest, padded - LANE, padded), BF16),
+            pltpu.VMEM((farthest, padded - LANE, padded), BF16),
+            pltpu.VMEM((farthest, padded, LANE), F32),
+            pltpu.VMEM((farthest, padded - LANE, padded), F32),
             pltpu.VMEM((8, LANE), F32),
             pltpu.VMEM((n_occ, 8, LANE), F32),
             dma((chunks + 3,)),
@@ -550,8 +683,10 @@
             dma((chunks, chips)),
             dma((chunks, chips)),
             dma((chunks, chips)),
-            dma((len(pieces), n_occ - 1)),
-            dma((len(pieces), n_occ - 1)),
+            dma((len(pieces) + 1, n_occ - 1)),
+            dma((len(pieces) + 1, n_occ - 1)),
+            dma((farthest,)),
+            dma((farthest,)),
             dma((farthest,)),
             dma((farthest,)),
             dma((n_occ,)),

time: 122 us -> 117 us (0.959)
  the two profiles are of different devices: /device:TPU:30 before, /device:TPU:8 now
where the time goes in v3:
time: 117 us; the launch traced here: 116 us
  Pallas kernels  111 us (95%)
  between operations  3.05 us (3%)
  local copies, waits for them, and re-layouts  1.98 us (2%)
    pallas_call x1, Pallas kernels, pair_results(): pl.pallas_call(functools.partial(pair_kernel, n_aux, n_occ, pieces), in_s...  111 us

profile of v3, /device:TPU:8, one launch (start us, length us, event | category | flops | bytes accessed | tf_op | source)
XLA Modules:
  0.0 116.4 jit_solution(3298411946012230106)
XLA Ops:
  1.3 111.4 %shard_map.104 = (bf16[1,200,1600]{2,1,0:T(8,128)(2,1)}, f32[1]{0:T(128)}) custom-call(bf16[8,48,4096]{2,1,0:T(8,128)(2,1)} %bitcast.4, s32[1,8]{1,0:T(1,128)} %mu_ref.1, s32[1,8]{1,0:T(1,128)} %nu_ref.1, s32[1]{0:T(128)S(6)} %copy.13.count_ref, bf16[32,4096]{1,0:T(8,128)(2,1)} %bitcast.5, bf16[1600,1408]{1,0:T(8,128)(2,1)} %bitcast.3, s32[32]{0:T(128)} %order_ref.1, ...), custom_call_target="tpu_custom_call" | custom-call | flops 14394851328 | bytes 4505600 | tf_op jit(solution)/shard_map/pallas_call | solution.py:638
  112.7 2.0 %copy.14 = bf16[1,200,1600]{2,1,0:T(8,128)(2,1)} copy(bf16[1,200,1600]{2,1,0:T(8,128)(2,1)} %get-tuple-element.4) | data formatting | bytes 1280000

commit v4 on v3

--- a/solution.py
+++ b/solution.py
@@ -141,6 +141,7 @@
     evir_ref,
     amp_ref,
     energy_ref,
+    amp,
     blocks,
     occ,
     tall,
@@ -181,6 +182,8 @@
     meta_recv,
     data_send,
     data_recv,
+    single_send,
+    single_recv,
     pass_send,
     pass_recv,
     ring_send,
@@ -267,28 +270,33 @@
     def data_copy(q, d):
         to = near(d)
         return pltpu.make_async_remote_copy(
-            ext.at[q, pl.ds(2 * to, 3)],
-            got.at[odd, chip, q],
+            ext.at[q, pl.ds(2 * to, 2)],
+            got.at[odd, chip, q, pl.ds(0, 2)],
             data_send.at[q, d],
             data_recv.at[q, d],
             device_id={"aux": 2 * to + odd},
             device_id_type=MESH,
         )
 
+    def single_copy(parity, d):
+        to = near(d)
+        return pltpu.make_async_remote_copy(
+            ext.at[:, 2 * to + 2],
+            got.at[odd, chip, :, 2],
+            single_send.at[d],
+            single_recv.at[parity, d],
+            device_id={"aux": 2 * to + 1},
+            device_id_type=MESH,
+        )
+
     def keep_copy(q):
         return pltpu.make_async_copy(ext.at[q, pl.ds(2 * chip, 3)], got.at[odd, chip, q], keep_sem.at[q])
 
-    def pass_copy(q, d):
-        view = got.at[odd, back(d), q, pl.ds(1 - odd, 2)]
+    def pass_copy(d):
+        view = got.at[odd, back(d), :, pl.ds(0, 2)]
         return pltpu.make_async_remote_copy(
-            view, view, pass_send.at[q, d], pass_recv.at[q, d], device_id={"aux": mate}, device_id_type=MESH
-        )
-
-    pl.semaphore_wait(barrier, chips + n_occ - 1)
-
-    @pl.loop(1, chips)
-    def _(d):
-        meta_copy(d).start()
+            view, view, pass_send.at[d], pass_recv.at[d], device_id={"aux": mate}, device_id_type=MESH
+        )
 
     @pl.loop(0, chunks)
     def _(q):
@@ -298,13 +306,27 @@
         half_transform(slots, occ_count, q, blocks, mixer, spread, prods, ext)
         keep_copy(q).start()
 
+        @pl.when(q == 0)
+        def _():
+            pl.semaphore_wait(barrier, chips + n_occ - 1)
+
+            @pl.loop(1, chips)
+            def _(d):
+                meta_copy(d).start()
+
         @pl.loop(1, chips)
         def _(d):
             data_copy(q, d).start()
 
-    tiles[:, 2 * packs] = jnp.zeros((2, ROWS, LANE), BF16)
+    @pl.loop(1, chips)
+    def _(d):
+        meta_copy(d).wait_recv()
+
+    meta_pass().start()
+    tiles[:, 2 * packs] = jnp.zeros((2, slab, LANE), BF16)
     load_vir.wait()
-    for c in range(n_occ):
+
+    def block_vir(c):
         low = c * width // ROWS * ROWS
         high = -(-(c + 1) * width // ROWS) * ROWS
         off = c * width - low
@@ -313,48 +335,60 @@
             if padded > width:
                 rows = jnp.concatenate([rows, jnp.zeros((padded - width, LANE), F32)], axis=0)
             vir_t[c, :, w : w + LANE] = rows.astype(BF16)
+
+    for c in range(n_occ // 2):
+        block_vir(c)
+    meta_pass().wait_recv()
+    placing = pltpu.make_async_copy(metas, places, local_sem.at[chunks + 2])
+    placing.start()
+    for c in range(n_occ // 2, n_occ):
+        block_vir(c)
     erow[...] = evir_ref[...].reshape(1, nvir)
     for c in range(n_occ):
         eblock[c] = jnp.concatenate(
             [erow[:, c * width : (c + 1) * width], jnp.ones((1, eblock.shape[2] - width), F32)], axis=1
         )
 
-    @pl.loop(1, chips)
-    def _(d):
-        meta_copy(d).wait_recv()
-
-    meta_pass().start()
-    meta_pass().wait_recv()
-    placing = pltpu.make_async_copy(metas, places, local_sem.at[chunks + 2])
-    placing.start()
-
     for q in range(chunks):
         keep_copy(q).wait()
-        pass_copy(q, 0).start()
+    pass_copy(0).start()
     placing.wait()
 
-    left = left_half((ROWS, LANE))
-    batch_rows = n_aux * ROWS
-
-    def spread_out(q, parity, source):
-        for side in range(2):
+    left = left_half((slab, LANE))
+
+    halves = (half_y, half_x)
+
+    def spread_sides(d, parity, sides):
+        source = back(d)
+        for side, slot in sides:
             for s in range(packs):
-                tile = got[parity, source, q, odd + side, :, s * LANE : (s + 1) * LANE]
+                tile = got[parity, source, :, slot, :, s * LANE : (s + 1) * LANE].reshape(slab, LANE)
                 tiles[side, s] = tile
                 tiles[side, packs + s] = pltpu.roll(tile.astype(F32), SHELL, 1).astype(BF16)
-        rows = pl.ds(pl.multiple_of(q * batch_rows + (parity * chips + source) * ROWS, ROWS), ROWS)
+        rows = pl.ds(pl.multiple_of((2 * d + parity) * slab, ROWS), slab)
         for c in range(nu_tiles):
             one = places[parity, source, 0, 2 * c]
             two = places[parity, source, 0, 2 * c + 1]
-            columns = slice(c * LANE, (c + 1) * LANE)
-            half_y[rows, columns] = jnp.where(left, tiles[0, one], tiles[0, two])
-            half_x[rows, columns] = jnp.where(left, tiles[1, one], tiles[1, two])
+            for side, _ in sides:
+                halves[side][rows, c * LANE : (c + 1) * LANE] = jnp.where(left, tiles[side, one], tiles[side, two])
+
+    def spread_out(d, parity):
+        @pl.when(odd == 0)
+        def _():
+            spread_sides(d, parity, ((0, 0), (1, 1)))
+
+        @pl.when(odd == 1)
+        def _():
+            spread_sides(d, parity, ((0, 1),))
 
     way = 1 - 2 * odd
     whole = out_ring.shape[1]
     front = out_rest.shape[2]
     rest = (whole, padded - whole, 1)
 
+    def times(one, two):
+        return lax.dot_general(one, two, NT, preferred_element_type=F32)
+
     def pick_rows(t):
         for row, rows, sign in pieces + [rest]:
             lhs[row : row + rows, :] = vir_t[around(-sign * way * (t + 1)), row : row + rows, :]
@@ -364,35 +398,82 @@
 
     pick_rows(0)
 
-    @pl.loop(0, chunks)
-    def _(q):
-        spread_out(q, odd, chip)
-
-        @pl.loop(1, chips)
-        def _(d):
-            data_copy(q, d).wait_recv()
-            pass_copy(q, d).start()
-            spread_out(q, odd, back(d))
-
-        @pl.loop(0, chips)
-        def _(d):
-            pass_copy(q, d).wait_recv()
-            spread_out(q, 1 - odd, back(d))
-
-        rows = pl.ds(pl.multiple_of(q * batch_rows, ROWS), batch_rows)
-        wide[:, :batch_rows] = lax.dot_general(
-            lhs[...], half_y[rows, :], NT, preferred_element_type=F32
-        ).astype(BF16)
-
-        @pl.when(q == 0)
+    group = max(1, chips // 4)
+    group_rows = 2 * group * slab
+
+    def rows_of(k):
+        return pl.ds(pl.multiple_of(k * group_rows, group_rows), group_rows)
+
+    def add_products(k):
+        rows = rows_of(k)
+
+        @pl.when(k == 0)
         def _():
             for low, high in column_cuts(256):
-                own[:, low:high] = jnp.dot(wide[:, :batch_rows], half_x[rows, low:high], preferred_element_type=F32)
-
-        @pl.when(q > 0)
+                own[:, low:high] = jnp.dot(wide[:, rows], half_x[rows, low:high], preferred_element_type=F32)
+
+        @pl.when(k > 0)
         def _():
             for low, high in column_cuts(256):
-                own[:, low:high] += jnp.dot(wide[:, :batch_rows], half_x[rows, low:high], preferred_element_type=F32)
+                own[:, low:high] += jnp.dot(wide[:, rows], half_x[rows, low:high], preferred_element_type=F32)
+
+    @pl.loop(0, chips // group)
+    def _(k):
+        @pl.loop(0, group)
+        def _(step):
+            d = k * group + step
+
+            @pl.when(d == min(0, chips - 1))
+            def _():
+                @pl.when(odd == 0)
+                def _():
+                    single_copy(0, 0).start()
+
+                @pl.loop(1, chips)
+                def _(e):
+                    single_copy(odd, e).start()
+
+            @pl.when(d > 0)
+            def _():
+                @pl.loop(0, chunks)
+                def _(q):
+                    data_copy(q, d).wait_recv()
+
+                pass_copy(d).start()
+
+            spread_out(d, odd)
+
+            @pl.when(step > 0)
+            def _():
+                pass_copy(d - 1).wait_recv()
+                spread_out(d - 1, 1 - odd)
+
+        pass_copy(k * group + group - 1).wait_recv()
+        spread_out(k * group + group - 1, 1 - odd)
+        rows = rows_of(k)
+        wide[:, rows] = times(lhs[...], half_y[rows, :]).astype(BF16)
+
+        @pl.when(odd == 0)
+        def _():
+            add_products(k)
+
+    @pl.when(odd == 1)
+    def _():
+        @pl.loop(0, chips // group)
+        def _(k):
+            @pl.loop(0, group)
+            def _(step):
+                d = k * group + step
+                single_copy(0, d).wait_recv()
+                spread_sides(d, 0, ((1, 2),))
+
+                @pl.when(d > 0)
+                def _():
+                    single_copy(1, d).wait_recv()
+
+                spread_sides(d, 1, ((1, 2),))
+
+            add_products(k)
 
     def ring_copy(t, k):
         if k == len(pieces):
@@ -486,9 +567,6 @@
             device_id_type=MESH,
         )
 
-    def times(one, two):
-        return lax.dot_general(one, two, NT, preferred_element_type=F32)
-
     @pl.when(nearer_half)
     def _():
         out_lead[far] = times(total_u[...], vir_t[far_block, :LANE, :]).astype(BF16)
@@ -520,8 +598,10 @@
         end = min(c + 256, nvir)
         pair = times(total_u[...], vir[c:end, :])
         ratio = pair / (e_rows - erow[:, c:end])
-        amp_ref[0, :, c:end] = ratio[:width].astype(BF16)
+        amp[0, :, c:end] = ratio[:width].astype(BF16)
         total = total + folded(ratio * (2.0 * pair))
+    leaving = pltpu.make_async_copy(amp, amp_ref, local_sem.at[0])
+    leaving.start()
 
     block = times(total_u[...], vir_t[g])
     same = times(vir_t[g], total_u[...])
@@ -576,6 +656,7 @@
         total = total + parts[d]
     energy_ref[0] = jnp.sum(total) / (nvir * nvir)
 
+    leaving.wait()
     for d in range(1, n_occ):
         part_copy(d).wait_send()
     for d in range(1, farthest):
@@ -603,12 +684,21 @@
 
     @pl.loop(0, chunks)
     def _(q):
-        pass_copy(q, 0).wait_send()
-
         @pl.loop(1, chips)
         def _(d):
             data_copy(q, d).wait_send()
-            pass_copy(q, d).wait_send()
+
+    @pl.loop(0, chips)
+    def _(d):
+        pass_copy(d).wait_send()
+
+    @pl.when(odd == 0)
+    def _():
+        single_copy(0, 0).wait_send()
+
+    @pl.loop(1, chips)
+    def _(d):
+        single_copy(odd, d).wait_send()
 
 
 def pair_results(
@@ -627,9 +717,11 @@
     mixed = slots * occ_count
     whole = width // ROWS * ROWS
     front = -(-nu_w // (2 * LANE)) * LANE
-    cuts = [whole * k // (4 * ROWS) * ROWS for k in range(5)]
-    spans = [(low, high - low, sign) for low, high, sign in zip(cuts[:-1], cuts[1:], (1, 1, -1, -1))]
-    pieces = [spans[k] for k in (0, 2, 1, 3) if spans[k][1]]
+    middle = whole // (2 * ROWS) * ROWS
+    step = 32
+    ahead = [(row, min(step, middle - row), 1) for row in range(0, middle, step)]
+    behind = [(row, min(step, whole - row), -1) for row in range(middle, whole, step)]
+    pieces = [piece for both in zip(ahead, behind) for piece in both]
     vmem = pl.BlockSpec(memory_space=pltpu.VMEM)
     smem = pl.BlockSpec(memory_space=pltpu.SMEM)
     anywhere = pl.BlockSpec(memory_space=pl.ANY)
@@ -638,9 +730,10 @@
     return pl.pallas_call(
         functools.partial(pair_kernel, n_aux, n_occ, pieces),
         in_specs=[anywhere, smem, smem, smem, anywhere, anywhere, smem, smem, vmem],
-        out_specs=(vmem, smem),
+        out_specs=(anywhere, smem),
         out_shape=(jax.ShapeDtypeStruct((1, width, nvir), BF16), jax.ShapeDtypeStruct((1,), F32)),
         scratch_shapes=[
+            pltpu.VMEM((1, width, nvir), BF16),
             pltpu.VMEM((chunks, slots, ROWS, SHELL * SHELL), BF16),
             pltpu.VMEM((occ_count, nao), BF16),
             pltpu.VMEM((slots * SHELL, mixed), F32),
@@ -652,7 +745,7 @@
             pltpu.VMEM((8, LANE), I32),
             pltpu.VMEM((2, chips, 8, LANE), I32),
             pltpu.SMEM((2, chips, 8, LANE), I32),
-            pltpu.VMEM((2, slots + 1, ROWS, LANE), BF16),
+            pltpu.VMEM((2, slots + 1, slab, LANE), BF16),
             pltpu.VMEM((aux_rows, nu_w), BF16),
             pltpu.VMEM((aux_rows, nu_w), BF16),
             pltpu.VMEM((nvir, nu_w), BF16),
@@ -681,8 +774,10 @@
             dma((chips,)),
             dma((chunks, chips)),
             dma((chunks, chips)),
-            dma((chunks, chips)),
-            dma((chunks, chips)),
+            dma((chips,)),
+            dma((2, chips)),
+            dma((chips,)),
+            dma((chips,)),
             dma((len(pieces) + 1, n_occ - 1)),
             dma((len(pieces) + 1, n_occ - 1)),
             dma((farthest,)),

time: 117 us -> 114 us (0.974)
  the two profiles are of different devices: /device:TPU:8 before, /device:TPU:1 now
where the time goes in v4:
time: 114 us; the launch traced here: 113 us
  Pallas kernels  108 us (95%)
  between operations  3.05 us (3%)
  local copies, waits for them, and re-layouts  1.98 us (2%)
    pallas_call x1, Pallas kernels, pair_results(): pl.pallas_call(functools.partial(pair_kernel, n_aux, n_occ, pieces), in_s...  108 us

profile of v4, /device:TPU:1, one launch (start us, length us, event | category | flops | bytes accessed | tf_op | source)
XLA Modules:
  0.0 113.0 jit_solution(7461033553975855438)
XLA Ops:
  1.3 108.0 %shard_map.104 = (bf16[1,200,1600]{2,1,0:T(8,128)(2,1)}, f32[1]{0:T(128)}) custom-call(bf16[8,48,4096]{2,1,0:T(8,128)(2,1)} %bitcast.4, s32[1,8]{1,0:T(1,128)} %mu_ref.1, s32[1,8]{1,0:T(1,128)} %nu_ref.1, s32[1]{0:T(128)S(6)} %copy.13.count_ref, bf16[32,4096]{1,0:T(8,128)(2,1)} %bitcast.5, bf16[1600,1408]{1,0:T(8,128)(2,1)} %bitcast.3, s32[32]{0:T(128)} %order_ref.1, ...), custom_call_target="tpu_custom_call" | custom-call | flops 14394851328 | bytes 4505600 | tf_op jit(solution)/shard_map/pallas_call | solution.py:730
  109.3 2.0 %copy.14 = bf16[1,200,1600]{2,1,0:T(8,128)(2,1)} copy(bf16[1,200,1600]{2,1,0:T(8,128)(2,1)} %get-tuple-element.4) | data formatting | bytes 1280000

commit v5 on v4

--- a/solution.py
+++ b/solution.py
@@ -358,6 +358,9 @@
 
     halves = (half_y, half_x)
 
+    def own_or_not(parity):
+        return lax.rem(parity + odd, 2)
+
     def spread_sides(d, parity, sides):
         source = back(d)
         for side, slot in sides:
@@ -365,7 +368,7 @@
                 tile = got[parity, source, :, slot, :, s * LANE : (s + 1) * LANE].reshape(slab, LANE)
                 tiles[side, s] = tile
                 tiles[side, packs + s] = pltpu.roll(tile.astype(F32), SHELL, 1).astype(BF16)
-        rows = pl.ds(pl.multiple_of((2 * d + parity) * slab, ROWS), slab)
+        rows = pl.ds(pl.multiple_of((own_or_not(parity) * chips + d) * slab, ROWS), slab)
         for c in range(nu_tiles):
             one = places[parity, source, 0, 2 * c]
             two = places[parity, source, 0, 2 * c + 1]
@@ -398,8 +401,8 @@
 
     pick_rows(0)
 
-    group = max(1, chips // 4)
-    group_rows = 2 * group * slab
+    group = chips // 2
+    group_rows = group * slab
 
     def rows_of(k):
         return pl.ds(pl.multiple_of(k * group_rows, group_rows), group_rows)
@@ -417,21 +420,27 @@
             for low, high in column_cuts(256):
                 own[:, low:high] += jnp.dot(wide[:, rows], half_x[rows, low:high], preferred_element_type=F32)
 
-    @pl.loop(0, chips // group)
+    def widen(k):
+        rows = rows_of(k)
+        wide[:, rows] = times(lhs[...], half_y[rows, :]).astype(BF16)
+
+        @pl.when(odd == 0)
+        def _():
+            add_products(k)
+
+    @pl.when(odd == 0)
+    def _():
+        single_copy(0, 0).start()
+
+    @pl.loop(1, chips)
+    def _(d):
+        single_copy(odd, d).start()
+
+    @pl.loop(0, 2)
     def _(k):
         @pl.loop(0, group)
         def _(step):
             d = k * group + step
-
-            @pl.when(d == min(0, chips - 1))
-            def _():
-                @pl.when(odd == 0)
-                def _():
-                    single_copy(0, 0).start()
-
-                @pl.loop(1, chips)
-                def _(e):
-                    single_copy(odd, e).start()
 
             @pl.when(d > 0)
             def _():
@@ -443,23 +452,25 @@
 
             spread_out(d, odd)
 
-            @pl.when(step > 0)
+            @pl.when(k == 1)
             def _():
-                pass_copy(d - 1).wait_recv()
-                spread_out(d - 1, 1 - odd)
-
-        pass_copy(k * group + group - 1).wait_recv()
-        spread_out(k * group + group - 1, 1 - odd)
-        rows = rows_of(k)
-        wide[:, rows] = times(lhs[...], half_y[rows, :]).astype(BF16)
-
-        @pl.when(odd == 0)
-        def _():
-            add_products(k)
+                pass_copy(step).wait_recv()
+                spread_out(step, 1 - odd)
+
+        widen(k)
+
+    widen(2)
+
+    @pl.loop(group, chips)
+    def _(d):
+        pass_copy(d).wait_recv()
+        spread_out(d, 1 - odd)
+
+    widen(3)
 
     @pl.when(odd == 1)
     def _():
-        @pl.loop(0, chips // group)
+        @pl.loop(0, 2)
         def _(k):
             @pl.loop(0, group)
             def _(step):
@@ -474,6 +485,7 @@
                 spread_sides(d, 1, ((1, 2),))
 
             add_products(k)
+            add_products(k + 2)
 
     def ring_copy(t, k):
         if k == len(pieces):

time: 114 us -> 111 us (0.974)
  Pallas kernels: 108 us -> 105 us
    pallas_call x1, Pallas kernels: 108 us -> 105 us  [pair_results(): pl.pallas_call(functools.partial(pair_kernel, n_aux, n_occ, pieces), in_s...]
where the time goes in v5:
time: 111 us; the launch traced here: 110 us
  Pallas kernels  105 us (95%)
  between operations  3.05 us (3%)
  local copies, waits for them, and re-layouts  1.98 us (2%)
    pallas_call x1, Pallas kernels, pair_results(): pl.pallas_call(functools.partial(pair_kernel, n_aux, n_occ, pieces), in_s...  105 us

profile of v5, /device:TPU:1, one launch (start us, length us, event | category | flops | bytes accessed | tf_op | source)
XLA Modules:
  0.0 110.1 jit_solution(8107454143792604521)
XLA Ops:
  1.3 105.0 %shard_map.104 = (bf16[1,200,1600]{2,1,0:T(8,128)(2,1)}, f32[1]{0:T(128)}) custom-call(bf16[8,48,4096]{2,1,0:T(8,128)(2,1)} %bitcast.4, s32[1,8]{1,0:T(1,128)} %mu_ref.1, s32[1,8]{1,0:T(1,128)} %nu_ref.1, s32[1]{0:T(128)S(6)} %copy.13.count_ref, bf16[32,4096]{1,0:T(8,128)(2,1)} %bitcast.5, bf16[1600,1408]{1,0:T(8,128)(2,1)} %bitcast.3, s32[32]{0:T(128)} %order_ref.1, ...), custom_call_target="tpu_custom_call" | custom-call | flops 14394851328 | bytes 4505600 | tf_op jit(solution)/shard_map/pallas_call | solution.py:742
  106.3 2.0 %copy.14 = bf16[1,200,1600]{2,1,0:T(8,128)(2,1)} copy(bf16[1,200,1600]{2,1,0:T(8,128)(2,1)} %get-tuple-element.4) | data formatting | bytes 1280000

commit v6 on v5

--- a/solution.py
+++ b/solution.py
@@ -730,7 +730,7 @@
     whole = width // ROWS * ROWS
     front = -(-nu_w // (2 * LANE)) * LANE
     middle = whole // (2 * ROWS) * ROWS
-    step = 32
+    step = 48
     ahead = [(row, min(step, middle - row), 1) for row in range(0, middle, step)]
     behind = [(row, min(step, whole - row), -1) for row in range(middle, whole, step)]
     pieces = [piece for both in zip(ahead, behind) for piece in both]

time: 111 us -> 111 us (level)
  no operation moved by 1% of the time
where the time goes in v6:
time: 111 us; the launch traced here: 110 us
  Pallas kernels  105 us (95%)
  between operations  3.05 us (3%)
  local copies, waits for them, and re-layouts  1.98 us (2%)
    pallas_call x1, Pallas kernels, pair_results(): pl.pallas_call(functools.partial(pair_kernel, n_aux, n_occ, pieces), in_s...  105 us

profile of v6, /device:TPU:1, one launch (start us, length us, event | category | flops | bytes accessed | tf_op | source)
XLA Modules:
  0.0 109.8 jit_solution(5800121900580671976)
XLA Ops:
  1.3 104.8 %shard_map.104 = (bf16[1,200,1600]{2,1,0:T(8,128)(2,1)}, f32[1]{0:T(128)}) custom-call(bf16[8,48,4096]{2,1,0:T(8,128)(2,1)} %bitcast.4, s32[1,8]{1,0:T(1,128)} %mu_ref.1, s32[1,8]{1,0:T(1,128)} %nu_ref.1, s32[1]{0:T(128)S(6)} %copy.13.count_ref, bf16[32,4096]{1,0:T(8,128)(2,1)} %bitcast.5, bf16[1600,1408]{1,0:T(8,128)(2,1)} %bitcast.3, s32[32]{0:T(128)} %order_ref.1, ...), custom_call_target="tpu_custom_call" | custom-call | flops 14394851328 | bytes 4505600 | tf_op jit(solution)/shard_map/pallas_call | solution.py:742
  106.1 2.0 %copy.14 = bf16[1,200,1600]{2,1,0:T(8,128)(2,1)} copy(bf16[1,200,1600]{2,1,0:T(8,128)(2,1)} %get-tuple-element.4) | data formatting | bytes 1280000
